TPU v7x, 256 devices: a whole 4x4x8 slice. The times are simulated.
256 devices in a mesh: head: 32 (over y, x, core), blk: 8 (over z).
Axes of the slice: x: 4, y: 4, z: 8, core: 2. Of those that a mesh axis runs over, the one named last changes fastest.
Arguments:
- queries: bfloat16 [6144, 4096], P('blk', 'head'), may hold values from -10 to 10
- key_rows: bfloat16 [6144, 1024], P('blk', 'head'), may hold values from -10 to 10
- value_rows: bfloat16 [6144, 1024], P('blk', 'head'), may hold values from -4 to 4
- out_grad: bfloat16 [6144, 4096], P('blk', 'head'), may hold values from -1.5 to 1.5
- doc_lengths: int32 [16], replicated, may hold values from 1 to 1536, 6144 in all
Outputs:
- query_grad: bfloat16 [6144, 4096], P('blk', 'head')
- key_grad: bfloat16 [6144, 1024], P('blk', 'head')
- value_grad: bfloat16 [6144, 1024], P('blk', 'head')
Inputs may be any that keep to these rules, and one draw needn't show every extreme that they name: `doc_lengths`: they sum to 6144; the longest is exactly 1536.
All inputs are finite; a program needn't handle non-finite values.
Results may differ from a plain program's by a relative error of at most 0.0071.
Values may be sent and summed in bfloat16 or wider, within the bound.
A program may use at most 64 MiB of HBM per device.

v0:
```python
import jax
import jax.numpy as jnp
from jax import lax
from jax.sharding import PartitionSpec as P


def from_partner(array, axis, apart):
    return lax.ppermute(array, axis, [(i, i ^ 1 << apart) for i in range(lax.axis_size(axis))])


def shifted(block, axis, distance):
    devices = range(lax.axis_size(axis))
    route = [(i - distance, i) for i in devices if i - distance in devices]
    return lax.ppermute(block, axis, route)


def passed_along(block, axis, distance):
    devices = range(lax.axis_size(axis))
    route = [((i - distance) % len(devices), i) for i in devices]
    return lax.ppermute(block, axis, route)


def block_documents(doc_lengths, first_row, span_rows):
    doc_ends = jnp.cumsum(doc_lengths)
    positions = first_row + jnp.arange(span_rows, dtype=jnp.int32)
    doc_ids = jnp.sum((doc_ends[None, :] <= positions[:, None]).astype(jnp.int32), axis=1)
    return (positions, doc_ids)


def group_gather(pair):
    head_index = lax.axis_index("head")
    low_bit = head_index % 2
    high_bit = head_index // 2 % 2
    partner = from_partner(pair, "head", 0)
    half_pair = jnp.where(
        low_bit == 0,
        jnp.concatenate([pair, partner], axis=2),
        jnp.concatenate([partner, pair], axis=2),
    )
    partner_half = from_partner(half_pair, "head", 1)
    return jnp.where(
        high_bit == 0,
        jnp.concatenate([half_pair, partner_half], axis=2),
        jnp.concatenate([partner_half, half_pair], axis=2),
    )


def group_reduce(partials):
    head_index = lax.axis_index("head")
    low_bit = head_index % 2
    high_bit = head_index // 2 % 2
    half_width = partials.shape[2] // 2
    first_part = partials[:, :, :half_width]
    second_part = partials[:, :, half_width:]
    kept_part = jnp.where(high_bit == 0, first_part, second_part)
    outgoing = jnp.where(high_bit == 0, second_part, first_part)
    kept_part = kept_part + from_partner(outgoing, "head", 1)
    quarter_width = half_width // 2
    first_part = kept_part[:, :, :quarter_width]
    second_part = kept_part[:, :, quarter_width:]
    final_part = jnp.where(low_bit == 0, first_part, second_part)
    outgoing = jnp.where(low_bit == 0, second_part, first_part)
    return final_part + from_partner(outgoing, "head", 0)


def move_pair(pair):
    return shifted(pair, "blk", 1)


def move_sums(grad_sums, offset):
    return passed_along(grad_sums, "blk", offset)


def visible(pair):
    return group_gather(pair)


def shards(queries, key_rows, value_rows, out_grad, doc_lengths):
    rows = queries.shape[0]
    head_width = queries.shape[1]
    softmax_scale = head_width ** (-0.5)
    block_count = lax.axis_size("blk")
    own_block = lax.axis_index("blk")
    query_pos, query_docs = block_documents(doc_lengths, own_block * rows, rows)
    own_pair = jnp.stack([key_rows, value_rows])

    def tile_mask(key_block):
        key_pos, key_docs = block_documents(doc_lengths, key_block * rows, rows)
        allowed = (key_pos[None, :] <= query_pos[:, None]) & (
            key_docs[None, :] == query_docs[:, None]
        )
        is_live = (key_block == own_block) | (key_block < own_block) & (
            key_docs[rows - 1] == query_docs[0]
        )
        return (allowed, is_live)

    def tile_scores(whole_pair):
        return (
            jnp.einsum("id,jd->ij", queries, whole_pair[0], preferred_element_type=jnp.float32)
            * softmax_scale
        )

    def forward_tile(state, whole_pair, allowed):
        row_max, row_sum, out_sum = state
        masked = jnp.where(allowed, tile_scores(whole_pair), -jnp.inf)
        new_max = jnp.maximum(row_max, jnp.max(masked, axis=1))
        weights = jnp.exp(masked - new_max[:, None])
        factor = jnp.exp(row_max - new_max)
        row_sum = row_sum * factor + jnp.sum(weights, axis=1)
        product = jnp.dot(
            weights, whole_pair[1].astype(jnp.float32), precision=lax.Precision.HIGHEST
        )
        out_sum = out_sum * factor[:, None] + product
        return (new_max, row_sum, out_sum)

    def forward_step(state, travel_pair, key_block):
        whole_pair = visible(travel_pair)
        allowed, is_live = tile_mask(key_block)
        return forward_tile(state, whole_pair, allowed)

    state = (
        jnp.full((rows,), -jnp.inf, jnp.float32),
        jnp.zeros((rows,), jnp.float32),
        jnp.zeros((rows, head_width), jnp.float32),
    )
    state = forward_step(state, own_pair, own_block)

    def forward_loop(step, carry):
        travel_pair, inner = carry
        travel_pair = move_pair(travel_pair)
        key_block = (own_block - step) % block_count
        return (travel_pair, forward_step(inner, travel_pair, key_block))

    forward_carry = lax.fori_loop(1, block_count, forward_loop, (own_pair, state))
    row_max, row_sum, out_sum = forward_carry[1]
    log_norm = row_max + jnp.log(row_sum)
    attended = out_sum / row_sum[:, None]
    row_delta = jnp.sum(out_grad.astype(jnp.float32) * attended, axis=1)

    def backward_tile(query_sum, whole_pair, allowed):
        key_tile = whole_pair[0]
        value_tile = whole_pair[1]
        scores = tile_scores(whole_pair)
        weights = jnp.exp(jnp.where(allowed, scores - log_norm[:, None], -jnp.inf))
        weights_b = weights.astype(jnp.bfloat16)
        prob_grad = jnp.einsum(
            "id,jd->ij", out_grad, value_tile, preferred_element_type=jnp.float32
        )
        score_grad = (weights * (prob_grad - row_delta[:, None])).astype(jnp.bfloat16)
        query_sum = query_sum + jnp.dot(score_grad, key_tile, preferred_element_type=jnp.float32)
        key_part = jnp.einsum("ij,id->jd", score_grad, queries, preferred_element_type=jnp.float32)
        value_part = jnp.einsum(
            "ij,id->jd", weights_b, out_grad, preferred_element_type=jnp.float32
        )
        return (query_sum, jnp.stack([key_part, value_part]))

    def backward_step(query_sum, grad_sums, travel_pair, key_block):
        whole_pair = visible(travel_pair)
        allowed, is_live = tile_mask(key_block)
        query_sum, partials = backward_tile(query_sum, whole_pair, allowed)
        grad_sums = grad_sums + group_reduce(partials)
        return (query_sum, grad_sums)

    query_sum = jnp.zeros((rows, head_width), jnp.float32)
    grad_sums = jnp.zeros(own_pair.shape, jnp.float32)
    query_sum, grad_sums = backward_step(query_sum, grad_sums, own_pair, own_block)

    def backward_loop(step, carry):
        travel_pair, inner_query, inner_sums = carry
        travel_pair = move_pair(travel_pair)
        inner_sums = move_sums(inner_sums, 1)
        key_block = (own_block - step) % block_count
        inner_query, inner_sums = backward_step(inner_query, inner_sums, travel_pair, key_block)
        return (travel_pair, inner_query, inner_sums)

    backward_carry = lax.fori_loop(1, block_count, backward_loop, (own_pair, query_sum, grad_sums))
    query_sum = backward_carry[1]
    grad_sums = move_sums(backward_carry[2], (1 - block_count) % block_count)
    query_grad = (query_sum * softmax_scale).astype(jnp.bfloat16)
    key_grad = (grad_sums[0] * softmax_scale).astype(jnp.bfloat16)
    value_grad = grad_sums[1].astype(jnp.bfloat16)
    return (query_grad, key_grad, value_grad)


def solution(mesh):
    in_specs = (P("blk", "head"), P("blk", "head"), P("blk", "head"), P("blk", "head"), P())
    out_specs = (P("blk", "head"), P("blk", "head"), P("blk", "head"))
    return jax.shard_map(shards, mesh=mesh, in_specs=in_specs, out_specs=out_specs, check_vma=False)
```

profile of v0, /device:TPU:8, one launch (start us, length us, event | category | flops | bytes accessed | tf_op | source)
XLA Modules:
  0.0 552.9 jit_solution(11225600228474587586)
XLA Ops:
  5.5 5.6 %collective-permute-done.10 = bf16[2,768,64]{1,2,0:T(8,128)(2,1)S(1)} collective-permute-done((bf16[2,768,64]{1,2,0:T(8,128)(2,1)S(1)}, bf16[2,768,64]{1,2,0:T(8,128)(2,1)S(1)}, u32[]{:S(2)}, u32[]{:S(2)}) %collective-permute-start.10) | collective-permute-done | bytes 196640 | tf_op jit(solution)/shard_map/ppermute | solution.py:8
  13.0 2.5 fusion.18
  15.5 207.9 %while.44 = (s32[]{:T(128)}, bf16[2,768,32]{2,1,0:T(8,128)(2,1)S(1)}, f32[768]{0:T(1024)S(1)}, f32[768]{0:T(1024)S(1)}, f32[768,128]{1,0:T(8,128)S(1)}, /*index=...) while((s32[]{:T(128)}, ...), condition=%wide.region_8.9_spmd.clone, body=%wide.region_4.8_spmd.clone.sunk | while | flops 1065163072 | bytes 11483982 | solution.py:134
  15.5 4.0 collective-permute-start
  19.5 8.0 %collective-permute-done = bf16[2,768,32]{2,1,0:T(8,128)(2,1)S(1)} collective-permute-done((bf16[2,768,32]{2,1,0:T(8,128)(2,1)S(1)}, bf16[2,768,32]{2,1,0:T(8,128)(2,1)S(1)}, u32[]{:S(2)}, u32[]{:S(2)}) %collective-permute-start) | collective-permute-done | bytes 98336 | tf_op jit(solution)/shard_map/while/body/eval_jaxpr/ppermute | solution.py:14
  31.4 9.5 %collective-permute-done.2 = bf16[2,768,64]{2,1,0:T(8,128)(2,1)S(1)} collective-permute-done((bf16[2,768,64]{2,1,0:T(8,128)(2,1)S(1)}, bf16[2,768,64]{2,1,0:T(8,128)(2,1)S(1)}, u32[]{:S(2)}, u32[]{:S(2)}) %collective-permute-start.2) | collective-permute-done | bytes 196640 | tf_op jit(solution)/shard_map/while/body/eval_jaxpr/ppermute | solution.py:8
  44.6 4.4 collective-permute-start
  49.0 7.8 %collective-permute-done = bf16[2,768,32]{2,1,0:T(8,128)(2,1)S(1)} collective-permute-done((bf16[2,768,32]{2,1,0:T(8,128)(2,1)S(1)}, bf16[2,768,32]{2,1,0:T(8,128)(2,1)S(1)}, u32[]{:S(2)}, u32[]{:S(2)}) %collective-permute-start) | collective-permute-done | bytes 98336 | tf_op jit(solution)/shard_map/while/body/eval_jaxpr/ppermute | solution.py:14
  60.7 9.5 %collective-permute-done.2 = bf16[2,768,64]{2,1,0:T(8,128)(2,1)S(1)} collective-permute-done((bf16[2,768,64]{2,1,0:T(8,128)(2,1)S(1)}, bf16[2,768,64]{2,1,0:T(8,128)(2,1)S(1)}, u32[]{:S(2)}, u32[]{:S(2)}) %collective-permute-start.2) | collective-permute-done | bytes 196640 | tf_op jit(solution)/shard_map/while/body/eval_jaxpr/ppermute | solution.py:8
  73.9 4.4 collective-permute-start
  78.3 7.8 %collective-permute-done = bf16[2,768,32]{2,1,0:T(8,128)(2,1)S(1)} collective-permute-done((bf16[2,768,32]{2,1,0:T(8,128)(2,1)S(1)}, bf16[2,768,32]{2,1,0:T(8,128)(2,1)S(1)}, u32[]{:S(2)}, u32[]{:S(2)}) %collective-permute-start) | collective-permute-done | bytes 98336 | tf_op jit(solution)/shard_map/while/body/eval_jaxpr/ppermute | solution.py:14
  89.9 9.5 %collective-permute-done.2 = bf16[2,768,64]{2,1,0:T(8,128)(2,1)S(1)} collective-permute-done((bf16[2,768,64]{2,1,0:T(8,128)(2,1)S(1)}, bf16[2,768,64]{2,1,0:T(8,128)(2,1)S(1)}, u32[]{:S(2)}, u32[]{:S(2)}) %collective-permute-start.2) | collective-permute-done | bytes 196640 | tf_op jit(solution)/shard_map/while/body/eval_jaxpr/ppermute | solution.py:8
  103.1 4.4 collective-permute-start
  107.6 7.8 %collective-permute-done = bf16[2,768,32]{2,1,0:T(8,128)(2,1)S(1)} collective-permute-done((bf16[2,768,32]{2,1,0:T(8,128)(2,1)S(1)}, bf16[2,768,32]{2,1,0:T(8,128)(2,1)S(1)}, u32[]{:S(2)}, u32[]{:S(2)}) %collective-permute-start) | collective-permute-done | bytes 98336 | tf_op jit(solution)/shard_map/while/body/eval_jaxpr/ppermute | solution.py:14
  119.2 9.5 %collective-permute-done.2 = bf16[2,768,64]{2,1,0:T(8,128)(2,1)S(1)} collective-permute-done((bf16[2,768,64]{2,1,0:T(8,128)(2,1)S(1)}, bf16[2,768,64]{2,1,0:T(8,128)(2,1)S(1)}, u32[]{:S(2)}, u32[]{:S(2)}) %collective-permute-start.2) | collective-permute-done | bytes 196640 | tf_op jit(solution)/shard_map/while/body/eval_jaxpr/ppermute | solution.py:8
  132.4 5.1 collective-permute-start
  137.6 7.8 %collective-permute-done = bf16[2,768,32]{2,1,0:T(8,128)(2,1)S(1)} collective-permute-done((bf16[2,768,32]{2,1,0:T(8,128)(2,1)S(1)}, bf16[2,768,32]{2,1,0:T(8,128)(2,1)S(1)}, u32[]{:S(2)}, u32[]{:S(2)}) %collective-permute-start) | collective-permute-done | bytes 98336 | tf_op jit(solution)/shard_map/while/body/eval_jaxpr/ppermute | solution.py:14
  149.2 9.5 %collective-permute-done.2 = bf16[2,768,64]{2,1,0:T(8,128)(2,1)S(1)} collective-permute-done((bf16[2,768,64]{2,1,0:T(8,128)(2,1)S(1)}, bf16[2,768,64]{2,1,0:T(8,128)(2,1)S(1)}, u32[]{:S(2)}, u32[]{:S(2)}) %collective-permute-start.2) | collective-permute-done | bytes 196640 | tf_op jit(solution)/shard_map/while/body/eval_jaxpr/ppermute | solution.py:8
  162.4 5.6 %collective-permute-start = (bf16[2,768,32]{2,1,0:T(8,128)(2,1)S(1)}, bf16[2,768,32]{2,1,0:T(8,128)(2,1)S(1)}, u32[]{:S(2)}, u32[]{:S(2)}) collective-permute-start(bf16[2,768,32]{2,1,0:T(8,128)(2,1)S(1)} %get-tuple-element.941), channel_id=1, source_target_pairs={{0,1},{1,2},{2,3},{3,4},{4,5},{5,6},{6,7},{8,9},{9,10},{10,11},{11... | collective-permute-start | bytes 294920 | tf_op jit(solution)/shard_map/while/body/eval_jaxpr/ppermute | solution.py:14
  168.0 7.8 %collective-permute-done = bf16[2,768,32]{2,1,0:T(8,128)(2,1)S(1)} collective-permute-done((bf16[2,768,32]{2,1,0:T(8,128)(2,1)S(1)}, bf16[2,768,32]{2,1,0:T(8,128)(2,1)S(1)}, u32[]{:S(2)}, u32[]{:S(2)}) %collective-permute-start) | collective-permute-done | bytes 98336 | tf_op jit(solution)/shard_map/while/body/eval_jaxpr/ppermute | solution.py:14
  179.7 9.5 %collective-permute-done.2 = bf16[2,768,64]{2,1,0:T(8,128)(2,1)S(1)} collective-permute-done((bf16[2,768,64]{2,1,0:T(8,128)(2,1)S(1)}, bf16[2,768,64]{2,1,0:T(8,128)(2,1)S(1)}, u32[]{:S(2)}, u32[]{:S(2)}) %collective-permute-start.2) | collective-permute-done | bytes 196640 | tf_op jit(solution)/shard_map/while/body/eval_jaxpr/ppermute | solution.py:8
  192.9 5.6 %collective-permute-start = (bf16[2,768,32]{2,1,0:T(8,128)(2,1)S(1)}, bf16[2,768,32]{2,1,0:T(8,128)(2,1)S(1)}, u32[]{:S(2)}, u32[]{:S(2)}) collective-permute-start(bf16[2,768,32]{2,1,0:T(8,128)(2,1)S(1)} %get-tuple-element.941), channel_id=1, source_target_pairs={{0,1},{1,2},{2,3},{3,4},{4,5},{5,6},{6,7},{8,9},{9,10},{10,11},{11... | collective-permute-start | bytes 294920 | tf_op jit(solution)/shard_map/while/body/eval_jaxpr/ppermute | solution.py:14
  198.5 7.8 %collective-permute-done = bf16[2,768,32]{2,1,0:T(8,128)(2,1)S(1)} collective-permute-done((bf16[2,768,32]{2,1,0:T(8,128)(2,1)S(1)}, bf16[2,768,32]{2,1,0:T(8,128)(2,1)S(1)}, u32[]{:S(2)}, u32[]{:S(2)}) %collective-permute-start) | collective-permute-done | bytes 98336 | tf_op jit(solution)/shard_map/while/body/eval_jaxpr/ppermute | solution.py:14
  210.2 9.5 %collective-permute-done.2 = bf16[2,768,64]{2,1,0:T(8,128)(2,1)S(1)} collective-permute-done((bf16[2,768,64]{2,1,0:T(8,128)(2,1)S(1)}, bf16[2,768,64]{2,1,0:T(8,128)(2,1)S(1)}, u32[]{:S(2)}, u32[]{:S(2)}) %collective-permute-start.2) | collective-permute-done | bytes 196640 | tf_op jit(solution)/shard_map/while/body/eval_jaxpr/ppermute | solution.py:8
  223.4 2.8 convolution_bitcast_fusion.2
  230.8 9.0 %collective-permute-done.11 = f32[2,768,64]{1,2,0:T(8,128)S(1)} collective-permute-done((f32[2,768,64]{1,2,0:T(8,128)}, f32[2,768,64]{1,2,0:T(8,128)S(1)}, u32[]{:S(2)}, u32[]{:S(2)}) %collective-permute-start.11) | collective-permute-done | bytes 393248 | tf_op jit(solution)/shard_map/ppermute | solution.py:8
  241.5 298.9 %while.45 = (s32[]{:T(128)}, bf16[2,768,32]{2,1,0:T(8,128)(2,1)S(1)}, f32[768,128]{1,0:T(8,128)S(1)}, f32[2,768,32]{1,2,0:T(8,128)S(1)}, s32[]{:T(128)}, /*index...) while((s32[]{:T(128)}, ...), condition=%wide.region_12.13_spmd.clone, body=%wide.region_10.12_spmd.clone.sunk | while | flops 764547904 | bytes 24024020 | solution.py:176
  241.5 5.6 %collective-permute-start.3 = (bf16[2,768,32]{2,1,0:T(8,128)(2,1)S(1)}, bf16[2,768,32]{2,1,0:T(8,128)(2,1)S(1)}, u32[]{:S(2)}, u32[]{:S(2)}) collective-permute-start(bf16[2,768,32]{2,1,0:T(8,128)(2,1)S(1)} %get-tuple-element.1000), channel_id=1, source_target_pairs={{0,1},{1,2},{2,3},{3,4},{4,5},{5,6},{6,7},{8,9},{9,10},{10,11},{11... | collective-permute-start | bytes 294920 | tf_op jit(solution)/shard_map/while/body/eval_jaxpr/ppermute | solution.py:14
  247.2 8.6 %collective-permute-done.3 = bf16[2,768,32]{2,1,0:T(8,128)(2,1)S(1)} collective-permute-done((bf16[2,768,32]{2,1,0:T(8,128)(2,1)S(1)}, bf16[2,768,32]{2,1,0:T(8,128)(2,1)S(1)}, u32[]{:S(2)}, u32[]{:S(2)}) %collective-permute-start.3) | collective-permute-done | bytes 98336 | tf_op jit(solution)/shard_map/while/body/eval_jaxpr/ppermute | solution.py:14
  259.6 9.6 %collective-permute-done.5 = bf16[2,768,64]{2,1,0:T(8,128)(2,1)S(1)} collective-permute-done((bf16[2,768,64]{2,1,0:T(8,128)(2,1)S(1)}, bf16[2,768,64]{2,1,0:T(8,128)(2,1)S(1)}, u32[]{:S(2)}, u32[]{:S(2)}) %collective-permute-start.5) | collective-permute-done | bytes 196640 | tf_op jit(solution)/shard_map/while/body/eval_jaxpr/ppermute | solution.py:8
  273.6 3.7 collective-permute-start.6
  277.4 5.1 collective-permute-done.7
  284.2 5.6 %collective-permute-start.3 = (bf16[2,768,32]{2,1,0:T(8,128)(2,1)S(1)}, bf16[2,768,32]{2,1,0:T(8,128)(2,1)S(1)}, u32[]{:S(2)}, u32[]{:S(2)}) collective-permute-start(bf16[2,768,32]{2,1,0:T(8,128)(2,1)S(1)} %get-tuple-element.1000), channel_id=1, source_target_pairs={{0,1},{1,2},{2,3},{3,4},{4,5},{5,6},{6,7},{8,9},{9,10},{10,11},{11... | collective-permute-start | bytes 294920 | tf_op jit(solution)/shard_map/while/body/eval_jaxpr/ppermute | solution.py:14
  289.9 8.6 %collective-permute-done.3 = bf16[2,768,32]{2,1,0:T(8,128)(2,1)S(1)} collective-permute-done((bf16[2,768,32]{2,1,0:T(8,128)(2,1)S(1)}, bf16[2,768,32]{2,1,0:T(8,128)(2,1)S(1)}, u32[]{:S(2)}, u32[]{:S(2)}) %collective-permute-start.3) | collective-permute-done | bytes 98336 | tf_op jit(solution)/shard_map/while/body/eval_jaxpr/ppermute | solution.py:14
  302.3 9.6 %collective-permute-done.5 = bf16[2,768,64]{2,1,0:T(8,128)(2,1)S(1)} collective-permute-done((bf16[2,768,64]{2,1,0:T(8,128)(2,1)S(1)}, bf16[2,768,64]{2,1,0:T(8,128)(2,1)S(1)}, u32[]{:S(2)}, u32[]{:S(2)}) %collective-permute-start.5) | collective-permute-done | bytes 196640 | tf_op jit(solution)/shard_map/while/body/eval_jaxpr/ppermute | solution.py:8
  316.3 3.7 collective-permute-start.6
  320.1 5.1 collective-permute-done.7
  326.9 5.6 %collective-permute-start.3 = (bf16[2,768,32]{2,1,0:T(8,128)(2,1)S(1)}, bf16[2,768,32]{2,1,0:T(8,128)(2,1)S(1)}, u32[]{:S(2)}, u32[]{:S(2)}) collective-permute-start(bf16[2,768,32]{2,1,0:T(8,128)(2,1)S(1)} %get-tuple-element.1000), channel_id=1, source_target_pairs={{0,1},{1,2},{2,3},{3,4},{4,5},{5,6},{6,7},{8,9},{9,10},{10,11},{11... | collective-permute-start | bytes 294920 | tf_op jit(solution)/shard_map/while/body/eval_jaxpr/ppermute | solution.py:14
  332.6 8.6 %collective-permute-done.3 = bf16[2,768,32]{2,1,0:T(8,128)(2,1)S(1)} collective-permute-done((bf16[2,768,32]{2,1,0:T(8,128)(2,1)S(1)}, bf16[2,768,32]{2,1,0:T(8,128)(2,1)S(1)}, u32[]{:S(2)}, u32[]{:S(2)}) %collective-permute-start.3) | collective-permute-done | bytes 98336 | tf_op jit(solution)/shard_map/while/body/eval_jaxpr/ppermute | solution.py:14
  345.0 9.6 %collective-permute-done.5 = bf16[2,768,64]{2,1,0:T(8,128)(2,1)S(1)} collective-permute-done((bf16[2,768,64]{2,1,0:T(8,128)(2,1)S(1)}, bf16[2,768,64]{2,1,0:T(8,128)(2,1)S(1)}, u32[]{:S(2)}, u32[]{:S(2)}) %collective-permute-start.5) | collective-permute-done | bytes 196640 | tf_op jit(solution)/shard_map/while/body/eval_jaxpr/ppermute | solution.py:8
  359.0 3.7 collective-permute-start.6
  362.8 5.1 collective-permute-done.7
  369.6 5.6 %collective-permute-start.3 = (bf16[2,768,32]{2,1,0:T(8,128)(2,1)S(1)}, bf16[2,768,32]{2,1,0:T(8,128)(2,1)S(1)}, u32[]{:S(2)}, u32[]{:S(2)}) collective-permute-start(bf16[2,768,32]{2,1,0:T(8,128)(2,1)S(1)} %get-tuple-element.1000), channel_id=1, source_target_pairs={{0,1},{1,2},{2,3},{3,4},{4,5},{5,6},{6,7},{8,9},{9,10},{10,11},{11... | collective-permute-start | bytes 294920 | tf_op jit(solution)/shard_map/while/body/eval_jaxpr/ppermute | solution.py:14
  375.3 8.6 %collective-permute-done.3 = bf16[2,768,32]{2,1,0:T(8,128)(2,1)S(1)} collective-permute-done((bf16[2,768,32]{2,1,0:T(8,128)(2,1)S(1)}, bf16[2,768,32]{2,1,0:T(8,128)(2,1)S(1)}, u32[]{:S(2)}, u32[]{:S(2)}) %collective-permute-start.3) | collective-permute-done | bytes 98336 | tf_op jit(solution)/shard_map/while/body/eval_jaxpr/ppermute | solution.py:14
  387.7 9.6 %collective-permute-done.5 = bf16[2,768,64]{2,1,0:T(8,128)(2,1)S(1)} collective-permute-done((bf16[2,768,64]{2,1,0:T(8,128)(2,1)S(1)}, bf16[2,768,64]{2,1,0:T(8,128)(2,1)S(1)}, u32[]{:S(2)}, u32[]{:S(2)}) %collective-permute-start.5) | collective-permute-done | bytes 196640 | tf_op jit(solution)/shard_map/while/body/eval_jaxpr/ppermute | solution.py:8
  401.8 3.7 collective-permute-start.6
  405.5 5.1 collective-permute-done.7
  412.3 5.6 %collective-permute-start.3 = (bf16[2,768,32]{2,1,0:T(8,128)(2,1)S(1)}, bf16[2,768,32]{2,1,0:T(8,128)(2,1)S(1)}, u32[]{:S(2)}, u32[]{:S(2)}) collective-permute-start(bf16[2,768,32]{2,1,0:T(8,128)(2,1)S(1)} %get-tuple-element.1000), channel_id=1, source_target_pairs={{0,1},{1,2},{2,3},{3,4},{4,5},{5,6},{6,7},{8,9},{9,10},{10,11},{11... | collective-permute-start | bytes 294920 | tf_op jit(solution)/shard_map/while/body/eval_jaxpr/ppermute | solution.py:14
  418.0 8.6 %collective-permute-done.3 = bf16[2,768,32]{2,1,0:T(8,128)(2,1)S(1)} collective-permute-done((bf16[2,768,32]{2,1,0:T(8,128)(2,1)S(1)}, bf16[2,768,32]{2,1,0:T(8,128)(2,1)S(1)}, u32[]{:S(2)}, u32[]{:S(2)}) %collective-permute-start.3) | collective-permute-done | bytes 98336 | tf_op jit(solution)/shard_map/while/body/eval_jaxpr/ppermute | solution.py:14
  430.4 9.6 %collective-permute-done.5 = bf16[2,768,64]{2,1,0:T(8,128)(2,1)S(1)} collective-permute-done((bf16[2,768,64]{2,1,0:T(8,128)(2,1)S(1)}, bf16[2,768,64]{2,1,0:T(8,128)(2,1)S(1)}, u32[]{:S(2)}, u32[]{:S(2)}) %collective-permute-start.5) | collective-permute-done | bytes 196640 | tf_op jit(solution)/shard_map/while/body/eval_jaxpr/ppermute | solution.py:8
  444.5 3.7 collective-permute-start.6
  448.2 5.1 collective-permute-done.7
  455.0 5.6 %collective-permute-start.3 = (bf16[2,768,32]{2,1,0:T(8,128)(2,1)S(1)}, bf16[2,768,32]{2,1,0:T(8,128)(2,1)S(1)}, u32[]{:S(2)}, u32[]{:S(2)}) collective-permute-start(bf16[2,768,32]{2,1,0:T(8,128)(2,1)S(1)} %get-tuple-element.1000), channel_id=1, source_target_pairs={{0,1},{1,2},{2,3},{3,4},{4,5},{5,6},{6,7},{8,9},{9,10},{10,11},{11... | collective-permute-start | bytes 294920 | tf_op jit(solution)/shard_map/while/body/eval_jaxpr/ppermute | solution.py:14
  460.7 8.6 %collective-permute-done.3 = bf16[2,768,32]{2,1,0:T(8,128)(2,1)S(1)} collective-permute-done((bf16[2,768,32]{2,1,0:T(8,128)(2,1)S(1)}, bf16[2,768,32]{2,1,0:T(8,128)(2,1)S(1)}, u32[]{:S(2)}, u32[]{:S(2)}) %collective-permute-start.3) | collective-permute-done | bytes 98336 | tf_op jit(solution)/shard_map/while/body/eval_jaxpr/ppermute | solution.py:14
  473.1 9.6 %collective-permute-done.5 = bf16[2,768,64]{2,1,0:T(8,128)(2,1)S(1)} collective-permute-done((bf16[2,768,64]{2,1,0:T(8,128)(2,1)S(1)}, bf16[2,768,64]{2,1,0:T(8,128)(2,1)S(1)}, u32[]{:S(2)}, u32[]{:S(2)}) %collective-permute-start.5) | collective-permute-done | bytes 196640 | tf_op jit(solution)/shard_map/while/body/eval_jaxpr/ppermute | solution.py:8
  487.2 3.7 collective-permute-start.6
  490.9 5.1 collective-permute-done.7
  497.7 5.6 %collective-permute-start.3 = (bf16[2,768,32]{2,1,0:T(8,128)(2,1)S(1)}, bf16[2,768,32]{2,1,0:T(8,128)(2,1)S(1)}, u32[]{:S(2)}, u32[]{:S(2)}) collective-permute-start(bf16[2,768,32]{2,1,0:T(8,128)(2,1)S(1)} %get-tuple-element.1000), channel_id=1, source_target_pairs={{0,1},{1,2},{2,3},{3,4},{4,5},{5,6},{6,7},{8,9},{9,10},{10,11},{11... | collective-permute-start | bytes 294920 | tf_op jit(solution)/shard_map/while/body/eval_jaxpr/ppermute | solution.py:14
  503.4 8.6 %collective-permute-done.3 = bf16[2,768,32]{2,1,0:T(8,128)(2,1)S(1)} collective-permute-done((bf16[2,768,32]{2,1,0:T(8,128)(2,1)S(1)}, bf16[2,768,32]{2,1,0:T(8,128)(2,1)S(1)}, u32[]{:S(2)}, u32[]{:S(2)}) %collective-permute-start.3) | collective-permute-done | bytes 98336 | tf_op jit(solution)/shard_map/while/body/eval_jaxpr/ppermute | solution.py:14
  515.8 9.6 %collective-permute-done.5 = bf16[2,768,64]{2,1,0:T(8,128)(2,1)S(1)} collective-permute-done((bf16[2,768,64]{2,1,0:T(8,128)(2,1)S(1)}, bf16[2,768,64]{2,1,0:T(8,128)(2,1)S(1)}, u32[]{:S(2)}, u32[]{:S(2)}) %collective-permute-start.5) | collective-permute-done | bytes 196640 | tf_op jit(solution)/shard_map/while/body/eval_jaxpr/ppermute | solution.py:8
  529.9 3.7 collective-permute-start.6
  533.6 5.1 collective-permute-done.7
  540.4 3.8 collective-permute-start.13
  544.9 6.7 %collective-permute-done.13 = f32[2,768,32]{1,2,0:T(8,128)S(1)} collective-permute-done((f32[2,768,32]{1,2,0:T(8,128)S(1)}, f32[2,768,32]{1,2,0:T(8,128)S(1)}, u32[]{:S(2)}, u32[]{:S(2)}) %collective-permute-start.13) | collective-permute-done | bytes 196640 | tf_op jit(solution)/shard_map/ppermute | solution.py:20
  (294 shorter events, 136.7 us)
Async XLA Ops:
  3.8 7.2 %collective-permute-start.10 = (bf16[2,768,64]{1,2,0:T(8,128)(2,1)S(1)}, bf16[2,768,64]{1,2,0:T(8,128)(2,1)S(1)}, u32[]{:S(2)}, u32[]{:S(2)}) collective-permute-start(bf16[2,768,64]{1,2,0:T(8,128)(2,1)S(1)} %maximum_select_fusion.5), channel_id=1, source_target_pairs={{0,16},{8,24},{16,0},{24,8},{32,48},{40,56},{48,32},{56,40},{64,80... | collective-permute-start | bytes 589832 | tf_op jit(solution)/shard_map/ppermute | solution.py:8
  15.5 12.0 %collective-permute-start = (bf16[2,768,32]{2,1,0:T(8,128)(2,1)S(1)}, bf16[2,768,32]{2,1,0:T(8,128)(2,1)S(1)}, u32[]{:S(2)}, u32[]{:S(2)}) collective-permute-start(bf16[2,768,32]{2,1,0:T(8,128)(2,1)S(1)} %get-tuple-element.941), channel_id=1, source_target_pairs={{0,1},{1,2},{2,3},{3,4},{4,5},{5,6},{6,7},{8,9},{9,10},{10,11},{11... | collective-permute-start | bytes 294920 | tf_op jit(solution)/shard_map/while/body/eval_jaxpr/ppermute | solution.py:14
  27.5 1.7 collective-permute-start.1
  29.7 11.2 %collective-permute-start.2 = (bf16[2,768,64]{2,1,0:T(8,128)(2,1)S(1)}, bf16[2,768,64]{2,1,0:T(8,128)(2,1)S(1)}, u32[]{:S(2)}, u32[]{:S(2)}) collective-permute-start(bf16[2,768,64]{2,1,0:T(8,128)(2,1)S(1)} %maximum_select_fusion.10), channel_id=1, source_target_pairs={{0,16},{8,24},{16,0},{24,8},{32,48},{40,56},{48,32},{56,40},{64,80... | collective-permute-start | bytes 589832 | tf_op jit(solution)/shard_map/while/body/eval_jaxpr/ppermute | solution.py:8
  44.6 12.2 %collective-permute-start = (bf16[2,768,32]{2,1,0:T(8,128)(2,1)S(1)}, bf16[2,768,32]{2,1,0:T(8,128)(2,1)S(1)}, u32[]{:S(2)}, u32[]{:S(2)}) collective-permute-start(bf16[2,768,32]{2,1,0:T(8,128)(2,1)S(1)} %get-tuple-element.941), channel_id=1, source_target_pairs={{0,1},{1,2},{2,3},{3,4},{4,5},{5,6},{6,7},{8,9},{9,10},{10,11},{11... | collective-permute-start | bytes 294920 | tf_op jit(solution)/shard_map/while/body/eval_jaxpr/ppermute | solution.py:14
  56.8 1.7 collective-permute-start.1
  59.0 11.2 %collective-permute-start.2 = (bf16[2,768,64]{2,1,0:T(8,128)(2,1)S(1)}, bf16[2,768,64]{2,1,0:T(8,128)(2,1)S(1)}, u32[]{:S(2)}, u32[]{:S(2)}) collective-permute-start(bf16[2,768,64]{2,1,0:T(8,128)(2,1)S(1)} %maximum_select_fusion.10), channel_id=1, source_target_pairs={{0,16},{8,24},{16,0},{24,8},{32,48},{40,56},{48,32},{56,40},{64,80... | collective-permute-start | bytes 589832 | tf_op jit(solution)/shard_map/while/body/eval_jaxpr/ppermute | solution.py:8
  73.9 12.2 %collective-permute-start = (bf16[2,768,32]{2,1,0:T(8,128)(2,1)S(1)}, bf16[2,768,32]{2,1,0:T(8,128)(2,1)S(1)}, u32[]{:S(2)}, u32[]{:S(2)}) collective-permute-start(bf16[2,768,32]{2,1,0:T(8,128)(2,1)S(1)} %get-tuple-element.941), channel_id=1, source_target_pairs={{0,1},{1,2},{2,3},{3,4},{4,5},{5,6},{6,7},{8,9},{9,10},{10,11},{11... | collective-permute-start | bytes 294920 | tf_op jit(solution)/shard_map/while/body/eval_jaxpr/ppermute | solution.py:14
  86.1 1.7 collective-permute-start.1
  88.2 11.2 %collective-permute-start.2 = (bf16[2,768,64]{2,1,0:T(8,128)(2,1)S(1)}, bf16[2,768,64]{2,1,0:T(8,128)(2,1)S(1)}, u32[]{:S(2)}, u32[]{:S(2)}) collective-permute-start(bf16[2,768,64]{2,1,0:T(8,128)(2,1)S(1)} %maximum_select_fusion.10), channel_id=1, source_target_pairs={{0,16},{8,24},{16,0},{24,8},{32,48},{40,56},{48,32},{56,40},{64,80... | collective-permute-start | bytes 589832 | tf_op jit(solution)/shard_map/while/body/eval_jaxpr/ppermute | solution.py:8
  103.1 12.2 %collective-permute-start = (bf16[2,768,32]{2,1,0:T(8,128)(2,1)S(1)}, bf16[2,768,32]{2,1,0:T(8,128)(2,1)S(1)}, u32[]{:S(2)}, u32[]{:S(2)}) collective-permute-start(bf16[2,768,32]{2,1,0:T(8,128)(2,1)S(1)} %get-tuple-element.941), channel_id=1, source_target_pairs={{0,1},{1,2},{2,3},{3,4},{4,5},{5,6},{6,7},{8,9},{9,10},{10,11},{11... | collective-permute-start | bytes 294920 | tf_op jit(solution)/shard_map/while/body/eval_jaxpr/ppermute | solution.py:14
  115.4 1.7 collective-permute-start.1
  117.5 11.2 %collective-permute-start.2 = (bf16[2,768,64]{2,1,0:T(8,128)(2,1)S(1)}, bf16[2,768,64]{2,1,0:T(8,128)(2,1)S(1)}, u32[]{:S(2)}, u32[]{:S(2)}) collective-permute-start(bf16[2,768,64]{2,1,0:T(8,128)(2,1)S(1)} %maximum_select_fusion.10), channel_id=1, source_target_pairs={{0,16},{8,24},{16,0},{24,8},{32,48},{40,56},{48,32},{56,40},{64,80... | collective-permute-start | bytes 589832 | tf_op jit(solution)/shard_map/while/body/eval_jaxpr/ppermute | solution.py:8
  132.4 13.0 %collective-permute-start = (bf16[2,768,32]{2,1,0:T(8,128)(2,1)S(1)}, bf16[2,768,32]{2,1,0:T(8,128)(2,1)S(1)}, u32[]{:S(2)}, u32[]{:S(2)}) collective-permute-start(bf16[2,768,32]{2,1,0:T(8,128)(2,1)S(1)} %get-tuple-element.941), channel_id=1, source_target_pairs={{0,1},{1,2},{2,3},{3,4},{4,5},{5,6},{6,7},{8,9},{9,10},{10,11},{11... | collective-permute-start | bytes 294920 | tf_op jit(solution)/shard_map/while/body/eval_jaxpr/ppermute | solution.py:14
  145.4 1.7 collective-permute-start.1
  147.5 11.2 %collective-permute-start.2 = (bf16[2,768,64]{2,1,0:T(8,128)(2,1)S(1)}, bf16[2,768,64]{2,1,0:T(8,128)(2,1)S(1)}, u32[]{:S(2)}, u32[]{:S(2)}) collective-permute-start(bf16[2,768,64]{2,1,0:T(8,128)(2,1)S(1)} %maximum_select_fusion.10), channel_id=1, source_target_pairs={{0,16},{8,24},{16,0},{24,8},{32,48},{40,56},{48,32},{56,40},{64,80... | collective-permute-start | bytes 589832 | tf_op jit(solution)/shard_map/while/body/eval_jaxpr/ppermute | solution.py:8
  162.4 13.4 %collective-permute-start = (bf16[2,768,32]{2,1,0:T(8,128)(2,1)S(1)}, bf16[2,768,32]{2,1,0:T(8,128)(2,1)S(1)}, u32[]{:S(2)}, u32[]{:S(2)}) collective-permute-start(bf16[2,768,32]{2,1,0:T(8,128)(2,1)S(1)} %get-tuple-element.941), channel_id=1, source_target_pairs={{0,1},{1,2},{2,3},{3,4},{4,5},{5,6},{6,7},{8,9},{9,10},{10,11},{11... | collective-permute-start | bytes 294920 | tf_op jit(solution)/shard_map/while/body/eval_jaxpr/ppermute | solution.py:14
  175.8 1.7 collective-permute-start.1
  178.0 11.2 %collective-permute-start.2 = (bf16[2,768,64]{2,1,0:T(8,128)(2,1)S(1)}, bf16[2,768,64]{2,1,0:T(8,128)(2,1)S(1)}, u32[]{:S(2)}, u32[]{:S(2)}) collective-permute-start(bf16[2,768,64]{2,1,0:T(8,128)(2,1)S(1)} %maximum_select_fusion.10), channel_id=1, source_target_pairs={{0,16},{8,24},{16,0},{24,8},{32,48},{40,56},{48,32},{56,40},{64,80... | collective-permute-start | bytes 589832 | tf_op jit(solution)/shard_map/while/body/eval_jaxpr/ppermute | solution.py:8
  192.9 13.4 %collective-permute-start = (bf16[2,768,32]{2,1,0:T(8,128)(2,1)S(1)}, bf16[2,768,32]{2,1,0:T(8,128)(2,1)S(1)}, u32[]{:S(2)}, u32[]{:S(2)}) collective-permute-start(bf16[2,768,32]{2,1,0:T(8,128)(2,1)S(1)} %get-tuple-element.941), channel_id=1, source_target_pairs={{0,1},{1,2},{2,3},{3,4},{4,5},{5,6},{6,7},{8,9},{9,10},{10,11},{11... | collective-permute-start | bytes 294920 | tf_op jit(solution)/shard_map/while/body/eval_jaxpr/ppermute | solution.py:14
  206.3 1.7 collective-permute-start.1
  208.5 11.2 %collective-permute-start.2 = (bf16[2,768,64]{2,1,0:T(8,128)(2,1)S(1)}, bf16[2,768,64]{2,1,0:T(8,128)(2,1)S(1)}, u32[]{:S(2)}, u32[]{:S(2)}) collective-permute-start(bf16[2,768,64]{2,1,0:T(8,128)(2,1)S(1)} %maximum_select_fusion.10), channel_id=1, source_target_pairs={{0,16},{8,24},{16,0},{24,8},{32,48},{40,56},{48,32},{56,40},{64,80... | collective-permute-start | bytes 589832 | tf_op jit(solution)/shard_map/while/body/eval_jaxpr/ppermute | solution.py:8
  229.3 10.5 %collective-permute-start.11 = (f32[2,768,64]{1,2,0:T(8,128)}, f32[2,768,64]{1,2,0:T(8,128)S(1)}, u32[]{:S(2)}, u32[]{:S(2)}) collective-permute-start(f32[2,768,64]{1,2,0:T(8,128)} %broadcast_select_fusion.1), channel_id=1, source_target_pairs={{0,16},{8,24},{16,0},{24,8},{32,48},{40,56},{48,32},{56,40},{64,80... | collective-permute-start | bytes 1179656 | tf_op jit(solution)/shard_map/ppermute | solution.py:8
  241.5 14.3 %collective-permute-start.3 = (bf16[2,768,32]{2,1,0:T(8,128)(2,1)S(1)}, bf16[2,768,32]{2,1,0:T(8,128)(2,1)S(1)}, u32[]{:S(2)}, u32[]{:S(2)}) collective-permute-start(bf16[2,768,32]{2,1,0:T(8,128)(2,1)S(1)} %get-tuple-element.1000), channel_id=1, source_target_pairs={{0,1},{1,2},{2,3},{3,4},{4,5},{5,6},{6,7},{8,9},{9,10},{10,11},{11... | collective-permute-start | bytes 294920 | tf_op jit(solution)/shard_map/while/body/eval_jaxpr/ppermute | solution.py:14
  255.7 1.7 collective-permute-start.4
  257.9 11.2 %collective-permute-start.5 = (bf16[2,768,64]{2,1,0:T(8,128)(2,1)S(1)}, bf16[2,768,64]{2,1,0:T(8,128)(2,1)S(1)}, u32[]{:S(2)}, u32[]{:S(2)}) collective-permute-start(bf16[2,768,64]{2,1,0:T(8,128)(2,1)S(1)} %maximum_select_fusion.12), channel_id=1, source_target_pairs={{0,16},{8,24},{16,0},{24,8},{32,48},{40,56},{48,32},{56,40},{64,80... | collective-permute-start | bytes 589832 | tf_op jit(solution)/shard_map/while/body/eval_jaxpr/ppermute | solution.py:8
  272.1 10.4 %collective-permute-start.7 = (f32[2,768,64]{1,2,0:T(8,128)S(1)}, f32[2,768,64]{1,2,0:T(8,128)S(1)}, u32[]{:S(2)}, u32[]{:S(2)}) collective-permute-start(f32[2,768,64]{1,2,0:T(8,128)S(1)} %broadcast_select_fusion.3), channel_id=1, source_target_pairs={{0,16},{8,24},{16,0},{24,8},{32,48},{40,56},{48,32},{56,40},{64,80... | collective-permute-start | bytes 1179656 | tf_op jit(solution)/shard_map/while/body/eval_jaxpr/ppermute | solution.py:8
  273.6 10.0 %collective-permute-start.6 = (f32[2,768,32]{1,2,0:T(8,128)S(1)}, f32[2,768,32]{1,2,0:T(8,128)S(1)}, u32[]{:S(2)}, u32[]{:S(2)}) collective-permute-start(f32[2,768,32]{1,2,0:T(8,128)S(1)} %get-tuple-element.1002), channel_id=1, source_target_pairs={{7,0},{0,1},{1,2},{2,3},{3,4},{4,5},{5,6},{6,7},{15,8},{8,9},{9,10... | collective-permute-start | bytes 589832 | tf_op jit(solution)/shard_map/while/body/eval_jaxpr/ppermute | solution.py:20
  284.2 14.3 %collective-permute-start.3 = (bf16[2,768,32]{2,1,0:T(8,128)(2,1)S(1)}, bf16[2,768,32]{2,1,0:T(8,128)(2,1)S(1)}, u32[]{:S(2)}, u32[]{:S(2)}) collective-permute-start(bf16[2,768,32]{2,1,0:T(8,128)(2,1)S(1)} %get-tuple-element.1000), channel_id=1, source_target_pairs={{0,1},{1,2},{2,3},{3,4},{4,5},{5,6},{6,7},{8,9},{9,10},{10,11},{11... | collective-permute-start | bytes 294920 | tf_op jit(solution)/shard_map/while/body/eval_jaxpr/ppermute | solution.py:14
  298.4 1.7 collective-permute-start.4
  300.6 11.2 %collective-permute-start.5 = (bf16[2,768,64]{2,1,0:T(8,128)(2,1)S(1)}, bf16[2,768,64]{2,1,0:T(8,128)(2,1)S(1)}, u32[]{:S(2)}, u32[]{:S(2)}) collective-permute-start(bf16[2,768,64]{2,1,0:T(8,128)(2,1)S(1)} %maximum_select_fusion.12), channel_id=1, source_target_pairs={{0,16},{8,24},{16,0},{24,8},{32,48},{40,56},{48,32},{56,40},{64,80... | collective-permute-start | bytes 589832 | tf_op jit(solution)/shard_map/while/body/eval_jaxpr/ppermute | solution.py:8
  314.8 10.4 %collective-permute-start.7 = (f32[2,768,64]{1,2,0:T(8,128)S(1)}, f32[2,768,64]{1,2,0:T(8,128)S(1)}, u32[]{:S(2)}, u32[]{:S(2)}) collective-permute-start(f32[2,768,64]{1,2,0:T(8,128)S(1)} %broadcast_select_fusion.3), channel_id=1, source_target_pairs={{0,16},{8,24},{16,0},{24,8},{32,48},{40,56},{48,32},{56,40},{64,80... | collective-permute-start | bytes 1179656 | tf_op jit(solution)/shard_map/while/body/eval_jaxpr/ppermute | solution.py:8
  316.3 10.0 %collective-permute-start.6 = (f32[2,768,32]{1,2,0:T(8,128)S(1)}, f32[2,768,32]{1,2,0:T(8,128)S(1)}, u32[]{:S(2)}, u32[]{:S(2)}) collective-permute-start(f32[2,768,32]{1,2,0:T(8,128)S(1)} %get-tuple-element.1002), channel_id=1, source_target_pairs={{7,0},{0,1},{1,2},{2,3},{3,4},{4,5},{5,6},{6,7},{15,8},{8,9},{9,10... | collective-permute-start | bytes 589832 | tf_op jit(solution)/shard_map/while/body/eval_jaxpr/ppermute | solution.py:20
  326.9 14.3 %collective-permute-start.3 = (bf16[2,768,32]{2,1,0:T(8,128)(2,1)S(1)}, bf16[2,768,32]{2,1,0:T(8,128)(2,1)S(1)}, u32[]{:S(2)}, u32[]{:S(2)}) collective-permute-start(bf16[2,768,32]{2,1,0:T(8,128)(2,1)S(1)} %get-tuple-element.1000), channel_id=1, source_target_pairs={{0,1},{1,2},{2,3},{3,4},{4,5},{5,6},{6,7},{8,9},{9,10},{10,11},{11... | collective-permute-start | bytes 294920 | tf_op jit(solution)/shard_map/while/body/eval_jaxpr/ppermute | solution.py:14
  341.1 1.7 collective-permute-start.4
  343.3 11.2 %collective-permute-start.5 = (bf16[2,768,64]{2,1,0:T(8,128)(2,1)S(1)}, bf16[2,768,64]{2,1,0:T(8,128)(2,1)S(1)}, u32[]{:S(2)}, u32[]{:S(2)}) collective-permute-start(bf16[2,768,64]{2,1,0:T(8,128)(2,1)S(1)} %maximum_select_fusion.12), channel_id=1, source_target_pairs={{0,16},{8,24},{16,0},{24,8},{32,48},{40,56},{48,32},{56,40},{64,80... | collective-permute-start | bytes 589832 | tf_op jit(solution)/shard_map/while/body/eval_jaxpr/ppermute | solution.py:8
  357.5 10.4 %collective-permute-start.7 = (f32[2,768,64]{1,2,0:T(8,128)S(1)}, f32[2,768,64]{1,2,0:T(8,128)S(1)}, u32[]{:S(2)}, u32[]{:S(2)}) collective-permute-start(f32[2,768,64]{1,2,0:T(8,128)S(1)} %broadcast_select_fusion.3), channel_id=1, source_target_pairs={{0,16},{8,24},{16,0},{24,8},{32,48},{40,56},{48,32},{56,40},{64,80... | collective-permute-start | bytes 1179656 | tf_op jit(solution)/shard_map/while/body/eval_jaxpr/ppermute | solution.py:8
  359.0 10.0 %collective-permute-start.6 = (f32[2,768,32]{1,2,0:T(8,128)S(1)}, f32[2,768,32]{1,2,0:T(8,128)S(1)}, u32[]{:S(2)}, u32[]{:S(2)}) collective-permute-start(f32[2,768,32]{1,2,0:T(8,128)S(1)} %get-tuple-element.1002), channel_id=1, source_target_pairs={{7,0},{0,1},{1,2},{2,3},{3,4},{4,5},{5,6},{6,7},{15,8},{8,9},{9,10... | collective-permute-start | bytes 589832 | tf_op jit(solution)/shard_map/while/body/eval_jaxpr/ppermute | solution.py:20
  368.0 1.5 collective-permute-start.8
  369.6 14.3 %collective-permute-start.3 = (bf16[2,768,32]{2,1,0:T(8,128)(2,1)S(1)}, bf16[2,768,32]{2,1,0:T(8,128)(2,1)S(1)}, u32[]{:S(2)}, u32[]{:S(2)}) collective-permute-start(bf16[2,768,32]{2,1,0:T(8,128)(2,1)S(1)} %get-tuple-element.1000), channel_id=1, source_target_pairs={{0,1},{1,2},{2,3},{3,4},{4,5},{5,6},{6,7},{8,9},{9,10},{10,11},{11... | collective-permute-start | bytes 294920 | tf_op jit(solution)/shard_map/while/body/eval_jaxpr/ppermute | solution.py:14
  383.9 1.7 collective-permute-start.4
  386.0 11.2 %collective-permute-start.5 = (bf16[2,768,64]{2,1,0:T(8,128)(2,1)S(1)}, bf16[2,768,64]{2,1,0:T(8,128)(2,1)S(1)}, u32[]{:S(2)}, u32[]{:S(2)}) collective-permute-start(bf16[2,768,64]{2,1,0:T(8,128)(2,1)S(1)} %maximum_select_fusion.12), channel_id=1, source_target_pairs={{0,16},{8,24},{16,0},{24,8},{32,48},{40,56},{48,32},{56,40},{64,80... | collective-permute-start | bytes 589832 | tf_op jit(solution)/shard_map/while/body/eval_jaxpr/ppermute | solution.py:8
  400.2 10.4 %collective-permute-start.7 = (f32[2,768,64]{1,2,0:T(8,128)S(1)}, f32[2,768,64]{1,2,0:T(8,128)S(1)}, u32[]{:S(2)}, u32[]{:S(2)}) collective-permute-start(f32[2,768,64]{1,2,0:T(8,128)S(1)} %broadcast_select_fusion.3), channel_id=1, source_target_pairs={{0,16},{8,24},{16,0},{24,8},{32,48},{40,56},{48,32},{56,40},{64,80... | collective-permute-start | bytes 1179656 | tf_op jit(solution)/shard_map/while/body/eval_jaxpr/ppermute | solution.py:8
  401.8 10.0 %collective-permute-start.6 = (f32[2,768,32]{1,2,0:T(8,128)S(1)}, f32[2,768,32]{1,2,0:T(8,128)S(1)}, u32[]{:S(2)}, u32[]{:S(2)}) collective-permute-start(f32[2,768,32]{1,2,0:T(8,128)S(1)} %get-tuple-element.1002), channel_id=1, source_target_pairs={{7,0},{0,1},{1,2},{2,3},{3,4},{4,5},{5,6},{6,7},{15,8},{8,9},{9,10... | collective-permute-start | bytes 589832 | tf_op jit(solution)/shard_map/while/body/eval_jaxpr/ppermute | solution.py:20
  410.7 1.5 collective-permute-start.8
  412.3 14.3 %collective-permute-start.3 = (bf16[2,768,32]{2,1,0:T(8,128)(2,1)S(1)}, bf16[2,768,32]{2,1,0:T(8,128)(2,1)S(1)}, u32[]{:S(2)}, u32[]{:S(2)}) collective-permute-start(bf16[2,768,32]{2,1,0:T(8,128)(2,1)S(1)} %get-tuple-element.1000), channel_id=1, source_target_pairs={{0,1},{1,2},{2,3},{3,4},{4,5},{5,6},{6,7},{8,9},{9,10},{10,11},{11... | collective-permute-start | bytes 294920 | tf_op jit(solution)/shard_map/while/body/eval_jaxpr/ppermute | solution.py:14
  426.6 1.7 collective-permute-start.4
  428.7 11.2 %collective-permute-start.5 = (bf16[2,768,64]{2,1,0:T(8,128)(2,1)S(1)}, bf16[2,768,64]{2,1,0:T(8,128)(2,1)S(1)}, u32[]{:S(2)}, u32[]{:S(2)}) collective-permute-start(bf16[2,768,64]{2,1,0:T(8,128)(2,1)S(1)} %maximum_select_fusion.12), channel_id=1, source_target_pairs={{0,16},{8,24},{16,0},{24,8},{32,48},{40,56},{48,32},{56,40},{64,80... | collective-permute-start | bytes 589832 | tf_op jit(solution)/shard_map/while/body/eval_jaxpr/ppermute | solution.py:8
  442.9 10.4 %collective-permute-start.7 = (f32[2,768,64]{1,2,0:T(8,128)S(1)}, f32[2,768,64]{1,2,0:T(8,128)S(1)}, u32[]{:S(2)}, u32[]{:S(2)}) collective-permute-start(f32[2,768,64]{1,2,0:T(8,128)S(1)} %broadcast_select_fusion.3), channel_id=1, source_target_pairs={{0,16},{8,24},{16,0},{24,8},{32,48},{40,56},{48,32},{56,40},{64,80... | collective-permute-start | bytes 1179656 | tf_op jit(solution)/shard_map/while/body/eval_jaxpr/ppermute | solution.py:8
  444.5 10.0 %collective-permute-start.6 = (f32[2,768,32]{1,2,0:T(8,128)S(1)}, f32[2,768,32]{1,2,0:T(8,128)S(1)}, u32[]{:S(2)}, u32[]{:S(2)}) collective-permute-start(f32[2,768,32]{1,2,0:T(8,128)S(1)} %get-tuple-element.1002), channel_id=1, source_target_pairs={{7,0},{0,1},{1,2},{2,3},{3,4},{4,5},{5,6},{6,7},{15,8},{8,9},{9,10... | collective-permute-start | bytes 589832 | tf_op jit(solution)/shard_map/while/body/eval_jaxpr/ppermute | solution.py:20
  453.4 1.5 collective-permute-start.8
  455.0 14.3 %collective-permute-start.3 = (bf16[2,768,32]{2,1,0:T(8,128)(2,1)S(1)}, bf16[2,768,32]{2,1,0:T(8,128)(2,1)S(1)}, u32[]{:S(2)}, u32[]{:S(2)}) collective-permute-start(bf16[2,768,32]{2,1,0:T(8,128)(2,1)S(1)} %get-tuple-element.1000), channel_id=1, source_target_pairs={{0,1},{1,2},{2,3},{3,4},{4,5},{5,6},{6,7},{8,9},{9,10},{10,11},{11... | collective-permute-start | bytes 294920 | tf_op jit(solution)/shard_map/while/body/eval_jaxpr/ppermute | solution.py:14
  469.3 1.7 collective-permute-start.4
  471.4 11.2 %collective-permute-start.5 = (bf16[2,768,64]{2,1,0:T(8,128)(2,1)S(1)}, bf16[2,768,64]{2,1,0:T(8,128)(2,1)S(1)}, u32[]{:S(2)}, u32[]{:S(2)}) collective-permute-start(bf16[2,768,64]{2,1,0:T(8,128)(2,1)S(1)} %maximum_select_fusion.12), channel_id=1, source_target_pairs={{0,16},{8,24},{16,0},{24,8},{32,48},{40,56},{48,32},{56,40},{64,80... | collective-permute-start | bytes 589832 | tf_op jit(solution)/shard_map/while/body/eval_jaxpr/ppermute | solution.py:8
  485.6 10.4 %collective-permute-start.7 = (f32[2,768,64]{1,2,0:T(8,128)S(1)}, f32[2,768,64]{1,2,0:T(8,128)S(1)}, u32[]{:S(2)}, u32[]{:S(2)}) collective-permute-start(f32[2,768,64]{1,2,0:T(8,128)S(1)} %broadcast_select_fusion.3), channel_id=1, source_target_pairs={{0,16},{8,24},{16,0},{24,8},{32,48},{40,56},{48,32},{56,40},{64,80... | collective-permute-start | bytes 1179656 | tf_op jit(solution)/shard_map/while/body/eval_jaxpr/ppermute | solution.py:8
  487.2 10.0 %collective-permute-start.6 = (f32[2,768,32]{1,2,0:T(8,128)S(1)}, f32[2,768,32]{1,2,0:T(8,128)S(1)}, u32[]{:S(2)}, u32[]{:S(2)}) collective-permute-start(f32[2,768,32]{1,2,0:T(8,128)S(1)} %get-tuple-element.1002), channel_id=1, source_target_pairs={{7,0},{0,1},{1,2},{2,3},{3,4},{4,5},{5,6},{6,7},{15,8},{8,9},{9,10... | collective-permute-start | bytes 589832 | tf_op jit(solution)/shard_map/while/body/eval_jaxpr/ppermute | solution.py:20
  496.1 1.5 collective-permute-start.8
  497.7 14.3 %collective-permute-start.3 = (bf16[2,768,32]{2,1,0:T(8,128)(2,1)S(1)}, bf16[2,768,32]{2,1,0:T(8,128)(2,1)S(1)}, u32[]{:S(2)}, u32[]{:S(2)}) collective-permute-start(bf16[2,768,32]{2,1,0:T(8,128)(2,1)S(1)} %get-tuple-element.1000), channel_id=1, source_target_pairs={{0,1},{1,2},{2,3},{3,4},{4,5},{5,6},{6,7},{8,9},{9,10},{10,11},{11... | collective-permute-start | bytes 294920 | tf_op jit(solution)/shard_map/while/body/eval_jaxpr/ppermute | solution.py:14
  512.0 1.7 collective-permute-start.4
  514.1 11.2 %collective-permute-start.5 = (bf16[2,768,64]{2,1,0:T(8,128)(2,1)S(1)}, bf16[2,768,64]{2,1,0:T(8,128)(2,1)S(1)}, u32[]{:S(2)}, u32[]{:S(2)}) collective-permute-start(bf16[2,768,64]{2,1,0:T(8,128)(2,1)S(1)} %maximum_select_fusion.12), channel_id=1, source_target_pairs={{0,16},{8,24},{16,0},{24,8},{32,48},{40,56},{48,32},{56,40},{64,80... | collective-permute-start | bytes 589832 | tf_op jit(solution)/shard_map/while/body/eval_jaxpr/ppermute | solution.py:8
  528.3 10.4 %collective-permute-start.7 = (f32[2,768,64]{1,2,0:T(8,128)S(1)}, f32[2,768,64]{1,2,0:T(8,128)S(1)}, u32[]{:S(2)}, u32[]{:S(2)}) collective-permute-start(f32[2,768,64]{1,2,0:T(8,128)S(1)} %broadcast_select_fusion.3), channel_id=1, source_target_pairs={{0,16},{8,24},{16,0},{24,8},{32,48},{40,56},{48,32},{56,40},{64,80... | collective-permute-start | bytes 1179656 | tf_op jit(solution)/shard_map/while/body/eval_jaxpr/ppermute | solution.py:8
  529.9 10.0 %collective-permute-start.6 = (f32[2,768,32]{1,2,0:T(8,128)S(1)}, f32[2,768,32]{1,2,0:T(8,128)S(1)}, u32[]{:S(2)}, u32[]{:S(2)}) collective-permute-start(f32[2,768,32]{1,2,0:T(8,128)S(1)} %get-tuple-element.1002), channel_id=1, source_target_pairs={{7,0},{0,1},{1,2},{2,3},{3,4},{4,5},{5,6},{6,7},{15,8},{8,9},{9,10... | collective-permute-start | bytes 589832 | tf_op jit(solution)/shard_map/while/body/eval_jaxpr/ppermute | solution.py:20
  538.8 1.5 collective-permute-start.8
  540.4 11.2 %collective-permute-start.13 = (f32[2,768,32]{1,2,0:T(8,128)S(1)}, f32[2,768,32]{1,2,0:T(8,128)S(1)}, u32[]{:S(2)}, u32[]{:S(2)}) collective-permute-start(f32[2,768,32]{1,2,0:T(8,128)S(1)} %get-tuple-element.626), channel_id=1, source_target_pairs={{7,0},{0,1},{1,2},{2,3},{3,4},{4,5},{5,6},{6,7},{15,8},{8,9},{9,10... | collective-permute-start | bytes 589832 | tf_op jit(solution)/shard_map/ppermute | solution.py:20
  (11 other events, 254.4 us)
where the time goes:
time: 557 us; the launch traced here: 553 us
  waiting for transfers between devices  337 us (61%)
  starting transfers between devices  140 us (25%)
  matrix products  48.5 us (9%)
  other arithmetic  23.9 us (4%)
    ppermute x46, waiting for transfers between devices, from_partner(): lax.ppermute(array, axis, [(i, i ^ 1 << apart) for i in range(lax.axis_si...  212 us
    ppermute x14, waiting for transfers between devices, shifted(): return lax.ppermute(block, axis, route)  115 us
    ppermute x14, starting transfers between devices, shifted(): return lax.ppermute(block, axis, route)  73 us
    ppermute x46, starting transfers between devices, from_partner(): lax.ppermute(array, axis, [(i, i ^ 1 << apart) for i in range(lax.axis_si...  37 us
    ppermute x8, starting transfers between devices, passed_along(): return lax.ppermute(block, axis, route)  29.7 us
    dot_general x8, matrix products, forward_tile(): jnp.dot(weights, whole_pair[1].astype(jnp.float32), precision=lax.Precisi...  17.3 us
    dot_general x15, matrix products, tile_scores(): jnp.einsum('id,jd->ij', queries, whole_pair[0], preferred_element_type=jn...  11.2 us
  transfers between devices with their start and end apart: 68, of which 68 were waited for; matrix products, arithmetic and copies ran while one was open for 2% of the time, Pallas kernels for 0%

commit v1 on v0

v1 whole, which is shorter than its diff:
```python
import functools

import jax
import jax.numpy as jnp
from jax import lax
from jax.experimental import pallas as pl
from jax.experimental.pallas import tpu as pltpu
from jax.sharding import PartitionSpec as P

f32, bf16 = jnp.float32, jnp.bfloat16
MESH = pl.DeviceIdType.MESH
LOG2E = 1.4426950408889634
BIG = 65536.0
SLOTS = 3


def dot(a, b):
    return jnp.dot(a, b, preferred_element_type=f32)


def dot_nt(a, b):
    return lax.dot_general(a, b, (((1,), (1,)), ((), ())), preferred_element_type=f32)


def kernel(
    blocks,
    doc_ref, q_hbm, k_hbm, v_hbm, do_hbm,
    dq_hbm, dk_hbm, dv_hbm,
    kv_in, qp, dop, kvt, p_s, ds_s, o_s, m_s, g_s, qst, dost, part, dq, dq_out, kv_out,
    pst, prc, xst, xrc, zst, zrc,
    load_sem, store_sem,
    z_send, z_recv, x_send, x_recv, p_send, p_recv, f_send, f_recv,
    rz_send, rz_recv, rx_send, rx_recv, rp_send, rp_recv,
):
    R, D = q_hbm.shape
    W = k_hbm.shape[1]
    T = R // 3
    scale = D ** -0.5
    C = scale * LOG2E
    head = lax.axis_index("head")
    blk = lax.axis_index("blk")
    core = lax.rem(head, 2)
    side = lax.rem(head // 2, 2)
    partner = {"head": head + 1 - 2 * core}
    across = {"head": head + 2 - 4 * side}
    up = {"blk": lax.rem(blk + 1, blocks)}
    down = {"blk": lax.rem(blk + blocks - 1, blocks)}
    q0 = 2 * side + core
    q1 = 2 * side + 1 - core
    q2 = 2 * (1 - side) + core
    q3 = 2 * (1 - side) + 1 - core

    def quarter(i):
        return pl.ds(pl.multiple_of(W * i, W), W)

    def remote(src, dst, send, recv, device):
        return pltpu.make_async_remote_copy(
            src_ref=src, dst_ref=dst, send_sem=send, recv_sem=recv,
            device_id=device, device_id_type=MESH,
        )

    barrier = pltpu.get_barrier_semaphore()
    for device in (partner, across, up, down):
        pl.semaphore_signal(barrier, inc=1, device_id=device, device_id_type=MESH)
    loads = [
        pltpu.make_async_copy(src, dst, load_sem.at[i])
        for i, (src, dst) in enumerate((
            (k_hbm, kv_in.at[0]), (v_hbm, kv_in.at[1]),
            (q_hbm, qp.at[:, 0:D]), (do_hbm, dop.at[:, 0:D]),
        ))
    ]
    for load in loads:
        load.start()
    for kv in range(2):
        loads[kv].wait()
        kvt[0, kv, quarter(q0), :] = kv_in[kv].astype(f32).T.astype(bf16)
    pl.semaphore_wait(barrier, 4)

    def rows(s, kv, i):
        return kvt.at[s, kv, quarter(i), :]

    def send_z(s, kv):
        return remote(rows(s, kv, q0), rows(s + 1, kv, q0), z_send.at[s, kv], z_recv.at[s, kv], up)

    def send_x(s, kv):
        return remote(rows(s, kv, q0), rows(s, kv, q0), x_send.at[s, kv], x_recv.at[s, kv], across)

    def send_p(s, kv):
        return remote(rows(s, kv, q0), rows(s, kv, q0), p_send.at[s, kv], p_recv.at[s, kv], partner)

    def send_f(s, kv):
        return remote(rows(s, kv, q2), rows(s, kv, q2), f_send.at[s, kv], f_recv.at[s, kv], partner)

    def landed(ref, sem):
        pltpu.make_async_copy(ref, ref, sem).wait()

    def spread(s, kv):
        if s < SLOTS - 1:
            send_z(s, kv).start()
        send_x(s, kv).start()
        send_p(s, kv).start()

    def pass_on(s):
        for kv in range(2):
            landed(rows(s, kv, q2), x_recv.at[s, kv])
            send_f(s, kv).start()

    def arrive(s):
        for kv in range(2):
            landed(rows(s, kv, q0), z_recv.at[s - 1, kv])
            spread(s, kv)

    def complete(s):
        for kv in range(2):
            landed(rows(s, kv, q1), p_recv.at[s, kv])
            landed(rows(s, kv, q3), f_recv.at[s, kv])

    for kv in range(2):
        spread(0, kv)

    starts, ends, total = [], [], jnp.int32(0)
    docs = doc_ref.shape[0]
    for n in range(docs):
        starts.append(total)
        total = total + doc_ref[n]
        ends.append(total)

    def bounds(shape, dim):
        n_of = lax.broadcasted_iota(jnp.int32, shape, dim)
        first = jnp.zeros(shape, jnp.int32)
        last = jnp.zeros(shape, jnp.int32)
        for n in range(docs):
            first = jnp.where(n_of == n, starts[n], first)
            last = jnp.where(n_of == n, ends[n], last)
        return first, last

    first, last = bounds((1, D), 1)
    pos = blk * R + lax.broadcasted_iota(jnp.int32, (R, D), 0)
    qp[:, D:] = jnp.where((pos >= first) & (pos < last), 1.0, 0.0).astype(bf16)
    first, last = bounds((docs, D), 0)
    first = jnp.concatenate([first] * (R // D), axis=1)
    last = jnp.concatenate([last] * (R // D), axis=1)
    for s in range(SLOTS):
        pos = lax.rem(blk + blocks - s, blocks) * R + lax.broadcasted_iota(jnp.int32, (docs, R), 1)
        kvt[s, 0, D:D + docs, :] = jnp.where((pos >= first) & (pos < last), 0.0, -BIG).astype(bf16)
        kvt[s, 0, D + docs:, :] = jnp.zeros((D - docs, R), bf16)
        kvt[s, 1, D:, :] = jnp.ones((D, R), bf16)

    def key_range(s, rt):
        return {0: (0, (rt + 1) * T), 1: (0, R), 2: (rt * T, R)}[s]

    def row_range(s, kt):
        return {0: (kt * T, R), 1: (0, R), 2: (0, (kt + 1) * T)}[s]

    def forward(s, rt):
        k0, k1 = key_range(s, rt)
        at = slice(rt * T, (rt + 1) * T)
        scores = dot(qp[at, :], kvt[s, 0, :, k0:k1])
        if s == 0:
            keep = lax.broadcasted_iota(jnp.int32, (T, T), 0) >= lax.broadcasted_iota(jnp.int32, (T, T), 1)
            diagonal = jnp.where(keep, scores[:, k1 - k0 - T:], -BIG)
            scores = diagonal if rt == 0 else jnp.concatenate([scores[:, :k1 - k0 - T], diagonal], axis=1)
        top = jnp.max(scores, axis=1, keepdims=True)
        weights = jnp.exp2((scores - top) * C).astype(bf16)
        p_s[s, at, k0:k1] = weights
        o_s[s, at, :] = dot_nt(weights, kvt[s, 1, :, k0:k1])
        m_s[s, at, :] = jnp.broadcast_to(top, (T, D))

    def combine(rt):
        at = slice(rt * T, (rt + 1) * T)
        tops = [m_s[s, at, :] for s in range(SLOTS)]
        top = functools.reduce(jnp.maximum, tops)
        factors = [jnp.exp2((x - top) * C) for x in tops]
        attended = sum(factors[s] * o_s[s, at, :D] for s in range(SLOTS))
        norm = sum(factors[s] * o_s[s, at, D:] for s in range(SLOTS))
        inverse = 1.0 / norm
        grad = dop[at, :D].astype(f32)
        query = qp[at, :D].astype(f32)
        left = -(jnp.sum(grad * attended, axis=1, keepdims=True) * inverse)
        lane = lax.broadcasted_iota(jnp.int32, (T, D), 1)
        terms = jnp.zeros((T, D), f32)
        for i in range(3):
            term = left.astype(bf16).astype(f32)
            left = left - term
            terms = jnp.where(lane == i, term, terms)
        dop[at, D:] = terms.astype(bf16)
        for s in range(SLOTS):
            factor = factors[s] * inverse
            g_s[s, at, :] = factor
            qst[s, :, at] = (query * factor).T.astype(bf16)
            dost[s, :, at] = (grad * factor).T.astype(bf16)

    def backward(s, kt):
        r0, r1 = row_range(s, kt)
        at = slice(kt * T, (kt + 1) * T)
        prob_grad = dot(dop[r0:r1, :], kvt[s, 1, :, at])
        weights = p_s[s, r0:r1, at]
        score_grad = (weights.astype(f32) * prob_grad).astype(bf16)
        ds_s[r0:r1, at] = score_grad
        part[s, 0, :, at] = dot(qst[s, :, r0:r1], score_grad)
        part[s, 1, :, at] = dot(dost[s, :, r0:r1], weights)

    def query_part(s, rt):
        k0, k1 = key_range(s, rt)
        at = slice(rt * T, (rt + 1) * T)
        x = dot_nt(ds_s[at, k0:k1], kvt[s, 0, :D, k0:k1]) * g_s[s, at, :]
        if s < SLOTS - 1:
            x = dq[at, :] + x
        if s == 0:
            dq_out[at, :] = (x * scale).astype(bf16)
        else:
            dq[at, :] = x

    def reduce_p(s, kv):
        return remote(pst.at[s, kv], prc.at[s, kv], rp_send.at[s, kv], rp_recv.at[s, kv], partner)

    def reduce_x(s, kv):
        return remote(xst.at[s, kv], xrc.at[s, kv], rx_send.at[s, kv], rx_recv.at[s, kv], across)

    def reduce_z(s, kv):
        return remote(zst.at[s - 1, kv], zrc.at[s - 1, kv], rz_send.at[s - 1, kv], rz_recv.at[s - 1, kv], down)

    def to_partner(s):
        for kv in range(2):
            for j in range(2):
                pst[s, kv, j] = part[s, kv, quarter(2 * j + 1 - core), :].astype(bf16)
            reduce_p(s, kv).start()

    def to_across(s):
        for kv in range(2):
            reduce_p(s, kv).wait_recv()
            xst[s, kv] = (part[s, kv, quarter(q2), :] + prc[s, kv, 1 - side].astype(f32)).astype(bf16)
            reduce_x(s, kv).start()

    def summed(s, kv):
        reduce_x(s, kv).wait_recv()
        total = part[s, kv, quarter(q0), :] + prc[s, kv, side].astype(f32) + xrc[s, kv].astype(f32)
        if s < SLOTS - 1:
            reduce_z(s + 1, kv).wait_recv()
            total = total + zrc[s, kv].astype(f32)
        return total

    def to_down(s):
        for kv in range(2):
            zst[s - 1, kv] = summed(s, kv).astype(bf16)
            reduce_z(s, kv).start()

    pass_on(0)
    arrive(1)
    for load in loads[2:]:
        load.wait()
    complete(0)
    for rt in range(3):
        forward(0, rt)
    pass_on(1)
    arrive(2)
    complete(1)
    for rt in range(3):
        forward(1, rt)
    pass_on(2)
    complete(2)
    for rt in range(3):
        forward(2, rt)
    for rt in range(3):
        combine(rt)

    for kt in range(3):
        backward(2, kt)
    to_partner(2)
    for rt in range(3):
        query_part(2, rt)
    backward(1, 0)
    to_across(2)
    backward(1, 1)
    backward(1, 2)
    to_partner(1)
    to_down(2)
    for rt in range(3):
        query_part(1, rt)
    backward(0, 0)
    to_across(1)
    backward(0, 1)
    backward(0, 2)
    to_partner(0)
    for rt in range(3):
        query_part(0, rt)
    dq_store = pltpu.make_async_copy(dq_out, dq_hbm, store_sem.at[2])
    dq_store.start()
    to_down(1)
    to_across(0)
    stores = [
        pltpu.make_async_copy(kv_out.at[kv], (dk_hbm, dv_hbm)[kv], store_sem.at[kv]) for kv in range(2)
    ]
    for kv in range(2):
        total = summed(0, kv)
        kv_out[kv] = ((total * scale) if kv == 0 else total).T.astype(bf16)
        stores[kv].start()

    for kv in range(2):
        for s in range(SLOTS):
            send_x(s, kv).wait_send()
            send_p(s, kv).wait_send()
            send_f(s, kv).wait_send()
            reduce_p(s, kv).wait_send()
            reduce_x(s, kv).wait_send()
        for s in range(SLOTS - 1):
            send_z(s, kv).wait_send()
            reduce_z(s + 1, kv).wait_send()
    for store in stores:
        store.wait()
    dq_store.wait()


def solution(mesh):
    blocks = mesh.shape["blk"]

    def shards(queries, key_rows, value_rows, out_grad, doc_lengths):
        R, D = queries.shape
        W = key_rows.shape[1]
        S = SLOTS
        hbm = pl.BlockSpec(memory_space=pl.ANY)
        vmem = pltpu.VMEM
        dma = pltpu.SemaphoreType.DMA
        flops = 2 * 6 * R * (7 * R // 3) * D
        return pl.pallas_call(
            functools.partial(kernel, blocks),
            out_shape=(
                jax.ShapeDtypeStruct((R, D), bf16),
                jax.ShapeDtypeStruct((R, W), bf16),
                jax.ShapeDtypeStruct((R, W), bf16),
            ),
            in_specs=[pl.BlockSpec(memory_space=pltpu.SMEM), hbm, hbm, hbm, hbm],
            out_specs=(hbm, hbm, hbm),
            scratch_shapes=[
                vmem((2, R, W), bf16), vmem((R, 2 * D), bf16), vmem((R, 2 * D), bf16),
                vmem((S, 2, 2 * D, R), bf16), vmem((S, R, R), bf16), vmem((R, R), bf16),
                vmem((S, R, 2 * D), f32), vmem((S, R, D), f32), vmem((S, R, D), f32),
                vmem((S, D, R), bf16), vmem((S, D, R), bf16), vmem((S, 2, D, R), f32),
                vmem((R, D), f32), vmem((R, D), bf16), vmem((2, R, W), bf16),
                vmem((S, 2, 2, W, R), bf16), vmem((S, 2, 2, W, R), bf16),
                vmem((S, 2, W, R), bf16), vmem((S, 2, W, R), bf16),
                vmem((S - 1, 2, W, R), bf16), vmem((S - 1, 2, W, R), bf16),
                dma((4,)), dma((3,)),
                dma((S - 1, 2)), dma((S - 1, 2)), dma((S, 2)), dma((S, 2)),
                dma((S, 2)), dma((S, 2)), dma((S, 2)), dma((S, 2)),
                dma((S - 1, 2)), dma((S - 1, 2)), dma((S, 2)), dma((S, 2)), dma((S, 2)), dma((S, 2)),
            ],
            compiler_params=pltpu.CompilerParams(
                collective_id=0, has_side_effects=True, vmem_limit_bytes=48 * 2**20,
            ),
            cost_estimate=pl.CostEstimate(flops=flops, bytes_accessed=4 * R * D * 2, transcendentals=R * R * 3),
        )(doc_lengths, queries, key_rows, value_rows, out_grad)

    specs = (P("blk", "head"),) * 4 + (P(),)
    return jax.shard_map(shards, mesh=mesh, in_specs=specs, out_specs=specs[:3], check_vma=False)
```

time: 557 us -> 39.1 us (0.07)
  waiting for transfers between devices: 337 us -> 0 us
  starting transfers between devices: 140 us -> 0 us
  matrix products: 48.5 us -> 0 us
  Pallas kernels: 0 us -> 34.5 us
  other arithmetic: 23.9 us -> 0 us
    ppermute x68 -> x0, waiting for transfers between devices: 337 us -> none  [the longest x46 212 us: from_partner(): lax.ppermute(array, axis, [(i, i ^ 1 << apart) for i in range(lax.axis_si...]
    ppermute x68 -> x0, starting transfers between devices: 140 us -> none  [the longest x14 73 us: shifted(): return lax.ppermute(block, axis, route)]
    dot_general x55 -> x0, matrix products: 48.5 us -> none  [the longest x8 17.3 us: forward_tile(): jnp.dot(weights, whole_pair[1].astype(jnp.float32), precision=lax.Precisi...]
    pallas_call x0 -> x1, Pallas kernels: none -> 34.5 us  [shards(): pl.pallas_call(functools.partial(kernel, blocks), out_shape=(jax.ShapeDty...]
    select_n x46 -> x0, other arithmetic: 14.5 us -> none  [the longest x15 7 us: group_gather(): jnp.where(low_bit == 0, jnp.concatenate([pair, partner], axis=2), jnp.con...]
  transfers between devices with their start and end apart: 68 -> 0, of which waited for: 68 -> 0; matrix products, arithmetic and copies ran while one was open for 2% -> 0% of each run, Pallas kernels for 0% -> 0%
where the time goes in v1:
time: 39.1 us; the launch traced here: 39 us
  Pallas kernels  34.5 us (88%)
  local copies, waits for them, and re-layouts  3.81 us (10%)
  between operations  0.7 us (2%)
    pallas_call x1, Pallas kernels, shards(): pl.pallas_call(functools.partial(kernel, blocks), out_shape=(jax.ShapeDty...  34.5 us
    unnamed x11, local copies, waits for them, and re-layouts  2.33 us
    pallas_call x2, local copies, waits for them, and re-layouts, shards(): pl.pallas_call(functools.partial(kernel, blocks), out_shape=(jax.ShapeDty...  1.49 us

profile of v1, /device:TPU:8, one launch (start us, length us, event | category | flops | bytes accessed | tf_op | source)
XLA Modules:
  0.0 39.0 jit_solution(430308156664208341)
XLA Ops:
  0.6 0.0 copy-start.1
  0.6 0.0 copy-start.3
  0.7 0.0 copy-start
  0.7 1.0 %copy.8.k_hbm = bf16[768,32]{1,0:T(8,128)(2,1)S(1)} copy(bf16[768,32]{0,1:T(8,128)(2,1)} %param.6) | data formatting | bytes 98304 | tf_op args[1]
  1.7 0.0 copy-done.3
  1.7 0.0 copy-start.2
  1.7 0.2 copy.9.v_hbm
  1.9 0.0 copy-done.1
  1.9 0.0 copy-done
  1.9 0.5 %copy-done.2 = s32[16]{0:T(128)S(1)} copy-done((s32[16]{0:T(128)S(1)}, s32[16]{0:T(128)}, u32[]{:S(2)}) %copy-start.2) | copy-done | bytes 88
  2.3 34.5 %shard_map.76 = (bf16[768,128]{1,0:T(8,128)(2,1)S(1)}, bf16[768,32]{1,0:T(8,128)(2,1)S(1)}, bf16[768,32]{1,0:T(8,128)(2,1)S(1)}) custom-call(s32[16]{0:T(128)S(1)} %copy-done.2, bf16[768,128]{1,0:T(8,128)(2,1)S(1)} %copy-done, bf16[768,32]{1,0:T(8,128)(2,1)S(1)} %copy.8.k_hbm, bf16[768,32]{1,0:T(8,128)(2,1)S(1)} %copy.9.v_hbm, bf16[768,128]{1,0:T(8,128)(2,1)S(1)} %copy-done.1), custom_call_target="tpu_custom_call" | custom-call | flops 2113929216 | bytes 786432 | tf_op jit(solution)/shard_map/pallas_call | solution.py:325
  36.9 0.7 %copy.10 = bf16[768,32]{0,1:T(8,128)(2,1)} copy(bf16[768,32]{1,0:T(8,128)(2,1)S(1)} %get-tuple-element.4) | data formatting | bytes 98304 | tf_op jit(solution)/shard_map/pallas_call | solution.py:325
  37.6 0.7 %copy.11 = bf16[768,32]{0,1:T(8,128)(2,1)} copy(bf16[768,32]{1,0:T(8,128)(2,1)S(1)} %get-tuple-element.5) | data formatting | bytes 98304 | tf_op jit(solution)/shard_map/pallas_call | solution.py:325
  38.4 0.7 %copy.13 = bf16[768,128]{1,0:T(8,128)(2,1)} copy(bf16[768,128]{1,0:T(8,128)(2,1)S(1)} %get-tuple-element.9) | data formatting | bytes 393216
Async XLA Ops:
  0.6 1.2 %copy-start.1 = (bf16[768,128]{1,0:T(8,128)(2,1)S(1)}, bf16[768,128]{1,0:T(8,128)(2,1)}, u32[]{:S(2)}) copy-start(bf16[768,128]{1,0:T(8,128)(2,1)} %do_hbm.1) | copy-start | bytes 589828
  0.6 1.0 %copy-start.3 = (bf16[768,32]{0,1:T(8,128)(2,1)S(1)}, bf16[768,32]{0,1:T(8,128)(2,1)}, u32[]{:S(2)}) copy-start(bf16[768,32]{0,1:T(8,128)(2,1)} %param.7) | copy-start | bytes 147460
  0.7 1.2 %copy-start = (bf16[768,128]{1,0:T(8,128)(2,1)S(1)}, bf16[768,128]{1,0:T(8,128)(2,1)}, u32[]{:S(2)}) copy-start(bf16[768,128]{1,0:T(8,128)(2,1)} %q_hbm.1) | copy-start | bytes 589828
  1.7 0.7 %copy-start.2 = (s32[16]{0:T(128)S(1)}, s32[16]{0:T(128)}, u32[]{:S(2)}) copy-start(s32[16]{0:T(128)} %doc_ref.1) | copy-start | bytes 196

commit v2 on v1

v2 whole, which is shorter than its diff:
```python
import functools

import jax
import jax.numpy as jnp
from jax import lax
from jax.experimental import pallas as pl
from jax.experimental.pallas import tpu as pltpu
from jax.sharding import PartitionSpec as P

f32, bf16 = jnp.float32, jnp.bfloat16
MESH = pl.DeviceIdType.MESH
LOG2E = 1.4426950408889634
BIG = 65536.0
CHUNKS = 2
SLOTS = 3


def dot(a, b):
    return jnp.dot(a, b, preferred_element_type=f32)


def dot_nt(a, b):
    return lax.dot_general(a, b, (((1,), (1,)), ((), ())), preferred_element_type=f32)


def kernel(
    blocks,
    doc_ref, q_hbm, k_hbm, v_hbm, do_hbm,
    dq_hbm, dk_hbm, dv_hbm,
    qp, dop, kvt, p_s, ds_s, o_s, l_s, m_s, g_s, qst, dost, part, dq, dq_out, kv_out,
    pst, prc, xst, xrc, zst, zrc,
    load_sem, store_sem,
    z_send, z_recv, d_send, d_recv, x_send, x_recv, p_send, p_recv, f_send, f_recv,
    rz_send, rz_recv, rd_send, rd_recv, rx_send, rx_recv, rp_send, rp_recv,
):
    R, D = q_hbm.shape
    W = k_hbm.shape[0]
    T = R // 3
    scale = D ** -0.5
    C = scale * LOG2E
    head = lax.axis_index("head")
    blk = lax.axis_index("blk")
    core = lax.rem(head, 2)
    side = lax.rem(head // 2, 2)
    partner = {"head": head + 1 - 2 * core}
    across = {"head": head + 2 - 4 * side}
    up = {"blk": lax.rem(blk + 1, blocks)}
    down = {"blk": lax.rem(blk + blocks - 1, blocks)}
    across_up, across_down = {**across, **up}, {**across, **down}
    q0 = 2 * side + core
    q1 = 2 * side + 1 - core
    q2 = 2 * (1 - side) + core
    q3 = 2 * (1 - side) + 1 - core

    def quarter(i):
        return pl.ds(pl.multiple_of(W * i, W), W)

    def chunk(c):
        return slice(c * (R // CHUNKS), (c + 1) * (R // CHUNKS))

    def tile(t):
        return slice(t * T, (t + 1) * T)

    def remote(src, dst, send, recv, device):
        return pltpu.make_async_remote_copy(
            src_ref=src, dst_ref=dst, send_sem=send, recv_sem=recv,
            device_id=device, device_id_type=MESH,
        )

    barrier = pltpu.get_barrier_semaphore()
    for device in (partner, across, up, down, across_up, across_down):
        pl.semaphore_signal(barrier, inc=1, device_id=device, device_id_type=MESH)
    kv_hbm = (k_hbm, v_hbm)
    loads = [
        pltpu.make_async_copy(src, dst, load_sem.at[i])
        for i, (src, dst) in enumerate((
            (k_hbm, kvt.at[0, 0, quarter(q0), :]), (v_hbm, kvt.at[0, 1, quarter(q0), :]),
            (q_hbm, qp.at[:, 0:D]), (do_hbm, dop.at[:, 0:D]),
        ))
    ]
    for load in loads:
        load.start()
    for load in loads[:2]:
        load.wait()
    pl.semaphore_wait(barrier, 6)

    def rows(s, kv, i, c):
        return kvt.at[s, kv, quarter(i), chunk(c)]

    def send_z(s, kv, c):
        return remote(rows(s, kv, q0, c), rows(s + 1, kv, q0, c), z_send, z_recv.at[s, kv, c], up)

    def send_d(kv, c):
        return remote(rows(1, kv, q0, c), rows(2, kv, q0, c), d_send, d_recv.at[kv, c], across_up)

    def send_x(s, kv, c):
        return remote(rows(s, kv, q0, c), rows(s, kv, q0, c), x_send, x_recv.at[s, kv, c], across)

    def send_p(s, kv, c):
        return remote(rows(s, kv, q0, c), rows(s, kv, q0, c), p_send, p_recv.at[s, kv, c], partner)

    def send_f(s, kv, c):
        return remote(rows(s, kv, q2, c), rows(s, kv, q2, c), f_send, f_recv.at[s, kv, c], partner)

    def landed(ref, sem):
        pltpu.make_async_copy(ref, ref, sem).wait()

    def spread(s, kv, c):
        if s < SLOTS - 1:
            send_z(s, kv, c).start()
            send_x(s, kv, c).start()
        if s == 1:
            send_d(kv, c).start()
        send_p(s, kv, c).start()

    def arrive(s, kv):
        for c in range(CHUNKS):
            landed(rows(s, kv, q0, c), z_recv.at[s - 1, kv, c])
            spread(s, kv, c)

    def pass_on(s, kv):
        for c in range(CHUNKS):
            landed(rows(s, kv, q2, c), x_recv.at[s, kv, c] if s < 2 else d_recv.at[kv, c])
            send_f(s, kv, c).start()

    def complete(s, kv):
        for c in range(CHUNKS):
            landed(rows(s, kv, q1, c), p_recv.at[s, kv, c])
            landed(rows(s, kv, q3, c), f_recv.at[s, kv, c])

    for kv in range(2):
        for c in range(CHUNKS):
            spread(0, kv, c)

    starts, ends, total = [], [], jnp.int32(0)
    docs = doc_ref.shape[0]
    for n in range(docs):
        starts.append(total)
        total = total + doc_ref[n]
        ends.append(total)

    def bounds(shape, dim):
        n_of = lax.broadcasted_iota(jnp.int32, shape, dim)
        first = jnp.zeros(shape, jnp.int32)
        last = jnp.zeros(shape, jnp.int32)
        for n in range(docs):
            first = jnp.where(n_of == n, starts[n], first)
            last = jnp.where(n_of == n, ends[n], last)
        return first, last

    first, last = bounds((1, D), 1)
    pos = blk * R + lax.broadcasted_iota(jnp.int32, (R, D), 0)
    qp[:, D:] = jnp.where((pos >= first) & (pos < last), 1.0, 0.0).astype(bf16)
    first, last = bounds((docs, D), 0)
    first = jnp.concatenate([first] * (R // D), axis=1)
    last = jnp.concatenate([last] * (R // D), axis=1)
    for s in range(SLOTS):
        pos = lax.rem(blk + blocks - s, blocks) * R + lax.broadcasted_iota(jnp.int32, (docs, R), 1)
        kvt[s, 0, D:D + docs, :] = jnp.where((pos >= first) & (pos < last), 0.0, -BIG).astype(bf16)
        kvt[s, 0, D + docs:, :] = jnp.zeros((D - docs, R), bf16)
        kvt[s, 1, D:, :] = jnp.ones((D, R), bf16)

    def key_range(s, rt):
        return {0: (0, (rt + 1) * T), 1: (0, R), 2: (rt * T, R)}[s]

    def row_range(s, kt):
        return {0: (kt * T, R), 1: (0, R), 2: (0, (kt + 1) * T)}[s]

    def weigh(s, rt):
        k0, k1 = key_range(s, rt)
        at = tile(rt)
        scores = dot(qp[at, :], kvt[s, 0, :, k0:k1])
        if s == 0:
            keep = lax.broadcasted_iota(jnp.int32, (T, T), 0) >= lax.broadcasted_iota(jnp.int32, (T, T), 1)
            diagonal = jnp.where(keep, scores[:, k1 - k0 - T:], -BIG)
            scores = diagonal if rt == 0 else jnp.concatenate([scores[:, :k1 - k0 - T], diagonal], axis=1)
        top = jnp.max(scores, axis=1, keepdims=True)
        weights = jnp.exp2((scores - top) * C).astype(bf16)
        p_s[s, at, k0:k1] = weights
        l_s[s, at, :] = dot_nt(weights, kvt[s, 1, D:, k0:k1])
        m_s[s, at, :] = jnp.broadcast_to(top, (T, D))

    def attend(s, rt):
        k0, k1 = key_range(s, rt)
        at = tile(rt)
        o_s[s, at, :] = dot_nt(p_s[s, at, k0:k1], kvt[s, 1, :D, k0:k1])

    def normalise(rt):
        at = tile(rt)
        tops = [m_s[s, at, :] for s in range(SLOTS)]
        top = functools.reduce(jnp.maximum, tops)
        factors = [jnp.exp2((x - top) * C) for x in tops]
        inverse = 1.0 / sum(factors[s] * l_s[s, at, :] for s in range(SLOTS))
        for s in range(SLOTS):
            g_s[s, at, :] = factors[s] * inverse

    def scaled(s, rt, source, target):
        at = tile(rt)
        target[s, :, at] = (source[at, :D].astype(f32) * g_s[s, at, :]).T.astype(bf16)

    def center(rt):
        at = tile(rt)
        attended = sum(g_s[s, at, :] * o_s[s, at, :] for s in range(SLOTS))
        left = -jnp.sum(dop[at, :D].astype(f32) * attended, axis=1, keepdims=True)
        lane = lax.broadcasted_iota(jnp.int32, (T, D), 1)
        terms = jnp.zeros((T, D), f32)
        for i in range(3):
            term = left.astype(bf16).astype(f32)
            left = left - term
            terms = jnp.where(lane == i, term, terms)
        dop[at, D:] = terms.astype(bf16)

    def value_part(s, kt):
        r0, r1 = row_range(s, kt)
        part[s, 1, :, tile(kt)] = dot(dost[s, :, r0:r1], p_s[s, r0:r1, tile(kt)])

    def key_part(s, kt):
        r0, r1 = row_range(s, kt)
        prob_grad = dot(dop[r0:r1, :], kvt[s, 1, :, tile(kt)])
        score_grad = (p_s[s, r0:r1, tile(kt)].astype(f32) * prob_grad).astype(bf16)
        ds_s[s, r0:r1, tile(kt)] = score_grad
        part[s, 0, :, tile(kt)] = dot(qst[s, :, r0:r1], score_grad)

    def query_part(s, rt):
        k0, k1 = key_range(s, rt)
        at = slice(rt * T, (rt + 1) * T)
        x = dot_nt(ds_s[s, at, k0:k1], kvt[s, 0, :D, k0:k1]) * g_s[s, at, :]
        if s < SLOTS - 1:
            x = dq[at, :] + x
        if s == 0:
            dq_out[at, :] = (x * scale).astype(bf16)
        else:
            dq[at, :] = x

    def reduce_p(s, kv, t):
        return remote(pst.at[s, kv, :, :, tile(t)], prc.at[s, kv, :, :, tile(t)], rp_send, rp_recv.at[s, kv, t], partner)

    def reduce_x(s, kv, t):
        return remote(xst.at[s, kv, :, tile(t)], xrc.at[s, kv, :, tile(t)], rx_send, rx_recv.at[s, kv, t], across)

    def reduce_d(kv, t):
        return remote(xst.at[2, kv, :, tile(t)], xrc.at[2, kv, :, tile(t)], rd_send, rd_recv.at[kv, t], across_down)

    def reduce_z(s, kv, t):
        return remote(zst.at[s - 1, kv, :, tile(t)], zrc.at[s - 1, kv, :, tile(t)], rz_send, rz_recv.at[s - 1, kv, t], down)

    def to_partner(s, kv, t):
        for j in range(2):
            pst[s, kv, j, :, tile(t)] = part[s, kv, quarter(2 * j + 1 - core), tile(t)].astype(bf16)
        reduce_p(s, kv, t).start()

    def to_across(s, kv):
        for t in range(3):
            reduce_p(s, kv, t).wait_recv()
            xst[s, kv, :, tile(t)] = (
                part[s, kv, quarter(q2), tile(t)] + prc[s, kv, 1 - side, :, tile(t)].astype(f32)
            ).astype(bf16)
            reduce_x(s, kv, t).start()

    def send_home(kv):
        for t in range(3):
            reduce_p(2, kv, t).wait_recv()
            xst[2, kv, :, tile(t)] = (
                part[2, kv, quarter(q2), tile(t)] + prc[2, kv, 1 - side, :, tile(t)].astype(f32)
            ).astype(bf16)
            reduce_d(kv, t).start()
            zst[1, kv, :, tile(t)] = (
                part[2, kv, quarter(q0), tile(t)] + prc[2, kv, side, :, tile(t)].astype(f32)
            ).astype(bf16)
            reduce_z(2, kv, t).start()

    def summed(s, kv, t):
        reduce_x(s, kv, t).wait_recv()
        total = (
            part[s, kv, quarter(q0), tile(t)] + prc[s, kv, side, :, tile(t)].astype(f32)
            + xrc[s, kv, :, tile(t)].astype(f32)
        )
        if s < SLOTS - 1:
            reduce_z(s + 1, kv, t).wait_recv()
            total = total + zrc[s, kv, :, tile(t)].astype(f32)
        if s == 1:
            reduce_d(kv, t).wait_recv()
            total = total + xrc[2, kv, :, tile(t)].astype(f32)
        return total

    def to_down(s, kv):
        for t in range(3):
            zst[s - 1, kv, :, tile(t)] = summed(s, kv, t).astype(bf16)
            reduce_z(s, kv, t).start()

    def values(s):
        for t in range(3):
            value_part(s, t)
            to_partner(s, 1, t)

    def keys(s):
        for t in range(3):
            key_part(s, t)
            to_partner(s, 0, t)

    def queries(s):
        for rt in range(3):
            query_part(s, rt)

    K, V = 0, 1
    for load in loads[2:]:
        load.wait()
    arrive(1, K)
    pass_on(0, K)
    arrive(1, V)
    pass_on(0, V)
    complete(0, K)
    for rt in range(3):
        weigh(0, rt)
    complete(0, V)
    for rt in range(3):
        attend(0, rt)
    pass_on(1, K)
    pass_on(1, V)
    arrive(2, K)
    pass_on(2, K)
    complete(1, K)
    for rt in range(3):
        weigh(1, rt)
    complete(2, K)
    for rt in range(3):
        weigh(2, rt)
    arrive(2, V)
    pass_on(2, V)
    for rt in range(3):
        normalise(rt)
        scaled(2, rt, dop, dost)
    values(2)
    for rt in range(3):
        scaled(1, rt, dop, dost)
    values(1)
    complete(1, V)
    for rt in range(3):
        attend(1, rt)
    send_home(V)
    for rt in range(3):
        scaled(0, rt, dop, dost)
    values(0)
    for rt in range(3):
        scaled(2, rt, qp, qst)
    complete(2, V)
    for rt in range(3):
        attend(2, rt)
        center(rt)
    keys(2)
    to_across(1, V)
    to_across(0, V)
    for rt in range(3):
        scaled(1, rt, qp, qst)
    keys(1)
    send_home(K)
    for rt in range(3):
        scaled(0, rt, qp, qst)
    keys(0)
    to_across(1, K)
    queries(2)
    to_across(0, K)
    queries(1)
    queries(0)
    dq_store = pltpu.make_async_copy(dq_out, dq_hbm, store_sem.at[2])
    dq_store.start()
    to_down(1, V)
    to_down(1, K)
    stores = [
        pltpu.make_async_copy(kv_out.at[kv], (dk_hbm, dv_hbm)[kv], store_sem.at[kv]) for kv in range(2)
    ]
    for kv in (V, K):
        for t in range(3):
            total = summed(0, kv, t)
            kv_out[kv, :, tile(t)] = (total * scale if kv == K else total).astype(bf16)
        stores[kv].start()

    landed(kvt.at[0:2, :, 0:W, :], x_send)
    landed(kvt.at[0, :, 0:W, :], d_send)
    landed(kvt.at[:, :, 0:W, :], p_send)
    landed(kvt.at[:, :, 0:W, :], f_send)
    landed(kvt.at[0:2, :, 0:W, :], z_send)
    landed(pst, rp_send)
    landed(xst.at[0:2], rx_send)
    landed(xst.at[2], rd_send)
    landed(zst, rz_send)
    for store in stores:
        store.wait()
    dq_store.wait()


def hand_over(*refs):
    copies = [pltpu.make_async_copy(refs[i], refs[3 + i], refs[6].at[i]) for i in range(3)]
    for copy in copies:
        copy.start()
    for copy in copies:
        copy.wait()


def solution(mesh):
    blocks = mesh.shape["blk"]

    def shards(queries, key_rows, value_rows, out_grad, doc_lengths):
        R, D = queries.shape
        W = key_rows.shape[1]
        S = SLOTS
        hbm = pl.BlockSpec(memory_space=pl.ANY)
        vmem = pltpu.VMEM
        dma = pltpu.SemaphoreType.DMA
        flops = 2 * 6 * R * (7 * R // 3) * D
        shapes = (
            jax.ShapeDtypeStruct((R, D), bf16),
            jax.ShapeDtypeStruct((W, R), bf16),
            jax.ShapeDtypeStruct((W, R), bf16),
        )
        grads = pl.pallas_call(
            functools.partial(kernel, blocks),
            out_shape=tuple(vmem(x.shape, x.dtype) for x in shapes),
            in_specs=[pl.BlockSpec(memory_space=pltpu.SMEM)] + [hbm] * 4,
            out_specs=(hbm, hbm, hbm),
            scratch_shapes=[
                vmem((R, 2 * D), bf16), vmem((R, 2 * D), bf16),
                vmem((S, 2, 2 * D, R), bf16), vmem((S, R, R), bf16), vmem((S, R, R), bf16),
                vmem((S, R, D), f32), vmem((S, R, D), f32), vmem((S, R, D), f32), vmem((S, R, D), f32),
                vmem((S, D, R), bf16), vmem((S, D, R), bf16), vmem((S, 2, D, R), f32),
                vmem((R, D), f32), vmem((R, D), bf16), vmem((2, W, R), bf16),
                vmem((S, 2, 2, W, R), bf16), vmem((S, 2, 2, W, R), bf16),
                vmem((S, 2, W, R), bf16), vmem((S, 2, W, R), bf16),
                vmem((S - 1, 2, W, R), bf16), vmem((S - 1, 2, W, R), bf16),
                dma((4,)), dma((3,)),
                dma, dma((S - 1, 2, CHUNKS)), dma, dma((2, CHUNKS)), dma, dma((S - 1, 2, CHUNKS)),
                dma, dma((S, 2, CHUNKS)), dma, dma((S, 2, CHUNKS)),
                dma, dma((S - 1, 2, 3)), dma, dma((2, 3)), dma, dma((S - 1, 2, 3)), dma, dma((S, 2, 3)),
            ],
            compiler_params=pltpu.CompilerParams(
                collective_id=0, has_side_effects=True, vmem_limit_bytes=60 * 2**20,
            ),
            cost_estimate=pl.CostEstimate(flops=flops, bytes_accessed=4 * R * D * 2, transcendentals=R * R * 3),
        )(doc_lengths, queries, key_rows.T, value_rows.T, out_grad)
        query_grad, key_grad, value_grad = pl.pallas_call(
            hand_over, out_shape=shapes, in_specs=[hbm] * 3, out_specs=(hbm,) * 3, scratch_shapes=[dma((3,))],
            compiler_params=pltpu.CompilerParams(vmem_limit_bytes=2 * 2**20),
        )(*grads)
        return query_grad, key_grad.T, value_grad.T

    specs = (P("blk", "head"),) * 4 + (P(),)
    return jax.shard_map(shards, mesh=mesh, in_specs=specs, out_specs=specs[:3], check_vma=False)
```

time: 39.1 us -> 33.1 us (0.85)
  local copies, waits for them, and re-layouts: 3.81 us -> 0 us
  Pallas kernels: 34.5 us -> 32.3 us
    unnamed x11 -> x0, local copies, waits for them, and re-layouts: 2.33 us -> none
    pallas_call x1 -> x2, Pallas kernels: 34.5 us -> 32.3 us  [the longest x1 31.6 us: shards(): pl.pallas_call(functools.partial(kernel, blocks), out_shape=tuple((vmem(x...]
    pallas_call x2 -> x0, local copies, waits for them, and re-layouts: 1.49 us -> none  [shards(): pl.pallas_call(functools.partial(kernel, blocks), out_shape=(jax.ShapeDty...]
where the time goes in v2:
time: 33.1 us; the launch traced here: 32.9 us
  Pallas kernels  32.3 us (98%)
  between operations  0.64 us (2%)
    pallas_call x1, Pallas kernels, shards(): pl.pallas_call(functools.partial(kernel, blocks), out_shape=tuple((vmem(x...  31.6 us
    pallas_call x1, Pallas kernels, shards(): pl.pallas_call(hand_over, out_shape=shapes, in_specs=[hbm] * 3, out_specs...  0.73 us

profile of v2, /device:TPU:8, one launch (start us, length us, event | category | flops | bytes accessed | tf_op | source)
XLA Modules:
  0.0 32.9 jit_solution(11794166127543751973)
XLA Ops:
  0.6 31.6 %shard_map.76 = (bf16[768,128]{1,0:T(8,128)(2,1)S(1)}, bf16[32,768]{1,0:T(8,128)(2,1)S(1)}, bf16[32,768]{1,0:T(8,128)(2,1)S(1)}) custom-call(s32[16]{0:T(128)} %doc_ref.1, bf16[768,128]{1,0:T(8,128)(2,1)} %q_hbm.1, bf16[32,768]{1,0:T(8,128)(2,1)} %bitcast.4, bf16[32,768]{1,0:T(8,128)(2,1)} %bitcast.5, bf16[768,128]{1,0:T(8,128)(2,1)} %do_hbm.1), custom_call_target="tpu_custom_call" | custom-call | flops 2113929216 | bytes 786432 | tf_op jit(solution)/shard_map/pallas_call | solution.py:416
  32.2 0.7 %shard_map.77 = (bf16[768,128]{1,0:T(8,128)(2,1)}, bf16[32,768]{1,0:T(8,128)(2,1)}, bf16[32,768]{1,0:T(8,128)(2,1)}) custom-call(bf16[768,128]{1,0:T(8,128)(2,1)S(1)} %get-tuple-element.9.refs_0_, bf16[32,768]{1,0:T(8,128)(2,1)S(1)} %get-tuple-element.10.refs_1_, bf16[32,768]{1,0:T(8,128)(2,1)S(1)} %get-tuple-element.11.refs_2_), custom_call_target="tpu_custom_call" | custom-call | tf_op jit(solution)/shard_map/pallas_call | solution.py:440

commit v3 on v2

v3 whole, which is shorter than its diff:
```python
import functools

import jax
import jax.numpy as jnp
from jax import lax
from jax.experimental import pallas as pl
from jax.experimental.pallas import tpu as pltpu
from jax.sharding import PartitionSpec as P

f32, bf16 = jnp.float32, jnp.bfloat16
MESH = pl.DeviceIdType.MESH
LOG2E = 1.4426950408889634
BIG = 65536.0
PARTS = 2
PIECES = 3
SLOTS = 3


def dot(a, b):
    return jnp.dot(a, b, preferred_element_type=f32)


def dot_nt(a, b):
    return lax.dot_general(a, b, (((1,), (1,)), ((), ())), preferred_element_type=f32)


def kernel(
    blocks,
    doc_hbm, q_hbm, k_hbm, v_hbm, do_hbm,
    dq_hbm, dk_hbm, dv_hbm,
    qp, do_in, kvt, p_s, w_s, ds_s, pg_s, e_s, l_s, m_s, g_s, delta, query_t, grad_t, part, dq, dq_out, kv_out,
    pst, prc, xst, xrc, zst, zrc,
    doc_ref, load_sem, store_sem,
    z_send, z_recv, d_send, d_recv, x_send, x_recv, p_send, p_recv, f_send, f_recv,
    rz_send, rz_recv, rd_send, rd_recv, rx_send, rx_recv, rp_send, rp_recv,
):
    R, D = q_hbm.shape
    W = k_hbm.shape[0]
    T = R // 3
    scale = D ** -0.5
    C = scale * LOG2E
    head = lax.axis_index("head")
    blk = lax.axis_index("blk")
    core = lax.rem(head, 2)
    side = lax.rem(head // 2, 2)
    partner = {"head": head + 1 - 2 * core}
    across = {"head": head + 2 - 4 * side}
    up = {"blk": lax.rem(blk + 1, blocks)}
    down = {"blk": lax.rem(blk + blocks - 1, blocks)}
    across_up, across_down = {**across, **up}, {**across, **down}
    q0 = 2 * side + core
    q1 = 2 * side + 1 - core
    q2 = 2 * (1 - side) + core
    q3 = 2 * (1 - side) + 1 - core

    def quarter(i):
        return pl.ds(pl.multiple_of(W * i, W), W)

    def cut(i, n):
        return slice(i * (R // n), (i + 1) * (R // n))

    def tile(t):
        return slice(t * T, (t + 1) * T)

    def remote(src, dst, send, recv, device):
        return pltpu.make_async_remote_copy(
            src_ref=src, dst_ref=dst, send_sem=send, recv_sem=recv,
            device_id=device, device_id_type=MESH,
        )

    barrier = pltpu.get_barrier_semaphore()
    for device in (partner, across, up, down, across_up, across_down):
        pl.semaphore_signal(barrier, inc=1, device_id=device, device_id_type=MESH)
    kv_hbm = (k_hbm, v_hbm)
    loads = [
        pltpu.make_async_copy(src, dst, load_sem.at[i])
        for i, (src, dst) in enumerate((
            (k_hbm, kvt.at[0, 0, quarter(q0), :]), (v_hbm, kvt.at[0, 1, quarter(q0), :]),
            (q_hbm, qp.at[:, 0:D]), (do_hbm, do_in), (doc_hbm, doc_ref),
        ))
    ]
    for load in loads:
        load.start()
    pl.semaphore_wait(barrier, 6)

    def rows(s, kv, i, c):
        return kvt.at[s, kv, quarter(i), cut(c, PARTS)]

    def own(s, kv, c):
        return kv_hbm[kv].at[:, cut(c, PARTS)] if s == 0 else rows(s, kv, q0, c)

    def send_z(s, kv, c):
        return remote(own(s, kv, c), rows(s + 1, kv, q0, c), z_send, z_recv.at[s, kv, c], up)

    def send_d(kv, c):
        return remote(rows(1, kv, q0, c), rows(2, kv, q0, c), d_send, d_recv.at[kv, c], across_up)

    def send_x(s, kv, c):
        return remote(own(s, kv, c), rows(s, kv, q0, c), x_send, x_recv.at[s, kv, c], across)

    def send_p(s, kv, c):
        return remote(own(s, kv, c), rows(s, kv, q0, c), p_send, p_recv.at[s, kv, c], partner)

    def send_f(s, kv, c):
        return remote(rows(s, kv, q2, c), rows(s, kv, q2, c), f_send, f_recv.at[s, kv, c], partner)

    def landed(ref, sem):
        pltpu.make_async_copy(ref, ref, sem).wait()

    def spread(s, kv, c):
        if s < SLOTS - 1:
            send_z(s, kv, c).start()
            send_x(s, kv, c).start()
        if s == 1:
            send_d(kv, c).start()
        send_p(s, kv, c).start()

    def arrive(s, kv):
        for c in range(PARTS):
            landed(rows(s, kv, q0, c), z_recv.at[s - 1, kv, c])
            spread(s, kv, c)

    def pass_on(s, kv):
        for c in range(PARTS):
            landed(rows(s, kv, q2, c), x_recv.at[s, kv, c] if s < 2 else d_recv.at[kv, c])
            send_f(s, kv, c).start()

    def complete(s, kv):
        if s == 0:
            loads[kv].wait()
        for c in range(PARTS):
            landed(rows(s, kv, q1, c), p_recv.at[s, kv, c])
            landed(rows(s, kv, q3, c), f_recv.at[s, kv, c])

    for kv in range(2):
        for c in range(PARTS):
            spread(0, kv, c)

    def prepare():
        loads[4].wait()
        starts, ends, total = [], [], jnp.int32(0)
        docs = doc_ref.shape[0]
        for n in range(docs):
            starts.append(total)
            total = total + doc_ref[n]
            ends.append(total)

        def bounds(shape, dim):
            n_of = lax.broadcasted_iota(jnp.int32, shape, dim)
            first = jnp.zeros(shape, jnp.int32)
            last = jnp.zeros(shape, jnp.int32)
            for n in range(docs):
                first = jnp.where(n_of == n, starts[n], first)
                last = jnp.where(n_of == n, ends[n], last)
            return first, last

        first, last = bounds((1, D), 1)
        pos = blk * R + lax.broadcasted_iota(jnp.int32, (R, D), 0)
        qp[:, D:] = jnp.where((pos >= first) & (pos < last), 1.0, 0.0).astype(bf16)
        first, last = bounds((docs, D), 0)
        first = jnp.concatenate([first] * (R // D), axis=1)
        last = jnp.concatenate([last] * (R // D), axis=1)
        for s in range(SLOTS):
            pos = lax.rem(blk + blocks - s, blocks) * R + lax.broadcasted_iota(jnp.int32, (docs, R), 1)
            kvt[s, 0, D:D + docs, :] = jnp.where((pos >= first) & (pos < last), 0.0, -BIG).astype(bf16)
            kvt[s, 0, D + docs:, :] = jnp.zeros((D - docs, R), bf16)
        for source, target, load in ((qp, query_t, loads[2]), (do_in, grad_t, loads[3])):
            load.wait()
            for rt in range(3):
                target[:, tile(rt)] = source[tile(rt), :D].astype(f32).T.astype(bf16)

    def key_range(s, rt):
        return {0: (0, (rt + 1) * T), 1: (0, R), 2: (rt * T, R)}[s]

    def row_range(s, kt):
        return {0: (kt * T, R), 1: (0, R), 2: (0, (kt + 1) * T)}[s]

    def row_tiles(s):
        return ((slice(0, R), slice(0, R)),) if s == 1 else tuple((tile(rt), slice(*key_range(s, rt))) for rt in range(3))

    def weigh(s):
        complete(s, 0)
        for at, keys in row_tiles(s):
            scores = dot(qp[at, :], kvt[s, 0, :, keys])
            if s == 0:
                keep = lax.broadcasted_iota(jnp.int32, (T, T), 0) >= lax.broadcasted_iota(jnp.int32, (T, T), 1)
                diagonal = jnp.where(keep, scores[:, keys.stop - T:], -BIG)
                scores = diagonal if keys.stop == T else jnp.concatenate([scores[:, :keys.stop - T], diagonal], axis=1)
            top = jnp.max(scores, axis=1, keepdims=True)
            weights = jnp.exp2((scores - top) * C)
            p_s[s, at, keys] = weights.astype(bf16)
            l_s[s, at, :] = jnp.broadcast_to(jnp.sum(weights, axis=1, keepdims=True), (at.stop - at.start, D))
            m_s[s, at, :] = jnp.broadcast_to(top, (at.stop - at.start, D))

    def slope(s):
        complete(s, 1)
        for at, keys in row_tiles(s):
            prob_grad = dot(do_in[at, :], kvt[s, 1, :D, keys])
            pg_s[s, at, keys] = prob_grad
            mean = jnp.sum(p_s[s, at, keys].astype(f32) * prob_grad, axis=1, keepdims=True)
            e_s[s, at, :] = jnp.broadcast_to(mean, (at.stop - at.start, D))

    def normalise():
        tops = [m_s[s] for s in range(SLOTS)]
        top = functools.reduce(jnp.maximum, tops)
        factors = [jnp.exp2((x - top) * C) for x in tops]
        inverse = 1.0 / sum(factors[s] * l_s[s] for s in range(SLOTS))
        for s in range(SLOTS):
            g_s[s] = factors[s] * inverse

    def center():
        delta[...] = sum(g_s[s] * e_s[s] for s in range(SLOTS))

    def across_lanes(x, keys):
        return jnp.concatenate([x] * ((keys.stop - keys.start) // D), axis=1)

    def values(s):
        for at, keys in row_tiles(s):
            w_s[s, at, keys] = (p_s[s, at, keys].astype(f32) * across_lanes(g_s[s, at, :], keys)).astype(bf16)
        for kt in range(3):
            r0, r1 = row_range(s, kt)
            part[s, 1, :, tile(kt)] = dot(grad_t[:, r0:r1], w_s[s, r0:r1, tile(kt)])
        to_partner(s, 1)

    def keys(s):
        for at, keys in row_tiles(s):
            score_grad = w_s[s, at, keys].astype(f32) * (pg_s[s, at, keys] - across_lanes(delta[at, :], keys))
            ds_s[s, at, keys] = score_grad.astype(bf16)
        for kt in range(3):
            r0, r1 = row_range(s, kt)
            part[s, 0, :, tile(kt)] = dot(query_t[:, r0:r1], ds_s[s, r0:r1, tile(kt)])
        to_partner(s, 0)

    def queries(s):
        for at, keys in row_tiles(s):
            x = dot_nt(ds_s[s, at, keys], kvt[s, 0, :D, keys])
            if s < SLOTS - 1:
                x = dq[at, :] + x
            if s == 0:
                dq_out[at, :] = (x * scale).astype(bf16)
            else:
                dq[at, :] = x

    def piece(t):
        return cut(t, PIECES)

    def reduce_p(s, kv, t):
        return remote(pst.at[s, kv, :, :, piece(t)], prc.at[s, kv, :, :, piece(t)], rp_send, rp_recv.at[s, kv, t], partner)

    def reduce_x(s, kv, t):
        return remote(xst.at[s, kv, :, piece(t)], xrc.at[s, kv, :, piece(t)], rx_send, rx_recv.at[s, kv, t], across)

    def reduce_d(kv, t):
        return remote(xst.at[2, kv, :, piece(t)], xrc.at[2, kv, :, piece(t)], rd_send, rd_recv.at[kv, t], across_down)

    def reduce_z(s, kv, t):
        return remote(zst.at[s - 1, kv, :, piece(t)], zrc.at[s - 1, kv, :, piece(t)], rz_send, rz_recv.at[s - 1, kv, t], down)

    def to_partner(s, kv):
        for t in range(PIECES):
            for j in range(2):
                pst[s, kv, j, :, piece(t)] = part[s, kv, quarter(2 * j + 1 - core), piece(t)].astype(bf16)
            reduce_p(s, kv, t).start()

    def of_pair(s, kv, t, i, j):
        return part[s, kv, quarter(i), piece(t)] + prc[s, kv, j, :, piece(t)].astype(f32)

    def to_across(s, kv):
        for t in range(PIECES):
            reduce_p(s, kv, t).wait_recv()
            xst[s, kv, :, piece(t)] = of_pair(s, kv, t, q2, 1 - side).astype(bf16)
            reduce_x(s, kv, t).start()

    def send_home(kv):
        for t in range(PIECES):
            reduce_p(2, kv, t).wait_recv()
            xst[2, kv, :, piece(t)] = of_pair(2, kv, t, q2, 1 - side).astype(bf16)
            reduce_d(kv, t).start()
            zst[1, kv, :, piece(t)] = of_pair(2, kv, t, q0, side).astype(bf16)
            reduce_z(2, kv, t).start()

    def summed(s, kv, t):
        reduce_x(s, kv, t).wait_recv()
        reduce_z(s + 1, kv, t).wait_recv()
        total = of_pair(s, kv, t, q0, side) + xrc[s, kv, :, piece(t)].astype(f32) + zrc[s, kv, :, piece(t)].astype(f32)
        if s == 1:
            reduce_d(kv, t).wait_recv()
            total = total + xrc[2, kv, :, piece(t)].astype(f32)
        return total

    def to_down(kv):
        for t in range(PIECES):
            zst[0, kv, :, piece(t)] = summed(1, kv, t).astype(bf16)
            reduce_z(1, kv, t).start()

    stores = [
        pltpu.make_async_copy(src, dst, store_sem.at[i])
        for i, (src, dst) in enumerate(((kv_out.at[0], dk_hbm), (kv_out.at[1], dv_hbm), (dq_out, dq_hbm)))
    ]

    def finish(kv):
        for t in range(PIECES):
            total = summed(0, kv, t)
            kv_out[kv, :, piece(t)] = (total * scale if kv == 0 else total).astype(bf16)
        stores[kv].start()

    K, V = 0, 1
    prepare()
    for kv in (K, V):
        arrive(1, kv)
        pass_on(0, kv)
    weigh(0)
    slope(0)
    pass_on(1, K)
    pass_on(1, V)
    arrive(2, K)
    pass_on(2, K)
    weigh(1)
    weigh(2)
    arrive(2, V)
    pass_on(2, V)
    normalise()
    values(2)
    slope(1)
    values(1)
    send_home(V)
    values(0)
    slope(2)
    center()
    keys(2)
    to_across(1, V)
    to_across(0, V)
    keys(1)
    send_home(K)
    keys(0)
    to_across(1, K)
    queries(2)
    to_across(0, K)
    queries(1)
    queries(0)
    stores[2].start()
    to_down(V)
    to_down(K)
    finish(V)
    finish(K)

    landed(kvt.at[0:2, :, 0:W, :], x_send)
    landed(kvt.at[0, :, 0:W, :], d_send)
    landed(kvt.at[:, :, 0:W, :], p_send)
    landed(kvt.at[:, :, 0:W, :], f_send)
    landed(kvt.at[0:2, :, 0:W, :], z_send)
    landed(pst, rp_send)
    landed(xst.at[0:2], rx_send)
    landed(xst.at[2], rd_send)
    landed(zst, rz_send)
    for store in stores:
        store.wait()


def hand_over(*refs):
    copies = [pltpu.make_async_copy(refs[i], refs[3 + i], refs[6].at[i]) for i in range(3)]
    for copy in copies:
        copy.start()
    for copy in copies:
        copy.wait()


def solution(mesh):
    blocks = mesh.shape["blk"]

    def shards(queries, key_rows, value_rows, out_grad, doc_lengths):
        R, D = queries.shape
        W = key_rows.shape[1]
        S = SLOTS
        hbm = pl.BlockSpec(memory_space=pl.ANY)
        vmem = pltpu.VMEM
        dma = pltpu.SemaphoreType.DMA
        flops = 2 * 6 * R * (7 * R // 3) * D
        shapes = (
            jax.ShapeDtypeStruct((R, D), bf16),
            jax.ShapeDtypeStruct((W, R), bf16),
            jax.ShapeDtypeStruct((W, R), bf16),
        )
        grads = pl.pallas_call(
            functools.partial(kernel, blocks),
            out_shape=tuple(vmem(x.shape, x.dtype) for x in shapes),
            in_specs=[hbm] * 5,
            out_specs=(hbm, hbm, hbm),
            scratch_shapes=[
                vmem((R, 2 * D), bf16), vmem((R, D), bf16),
                vmem((S, 2, 2 * D, R), bf16), vmem((S, R, R), bf16), vmem((S, R, R), bf16), vmem((S, R, R), bf16),
                vmem((S, R, R), f32), vmem((S, R, D), f32), vmem((S, R, D), f32), vmem((S, R, D), f32),
                vmem((S, R, D), f32), vmem((R, D), f32), vmem((D, R), bf16), vmem((D, R), bf16), vmem((S, 2, D, R), f32),
                vmem((R, D), f32), vmem((R, D), bf16), vmem((2, W, R), bf16),
                vmem((S, 2, 2, W, R), bf16), vmem((S, 2, 2, W, R), bf16),
                vmem((S, 2, W, R), bf16), vmem((S, 2, W, R), bf16),
                vmem((S - 1, 2, W, R), bf16), vmem((S - 1, 2, W, R), bf16),
                pltpu.SMEM((16,), jnp.int32), dma((5,)), dma((3,)),
                dma, dma((S - 1, 2, PARTS)), dma, dma((2, PARTS)), dma, dma((S - 1, 2, PARTS)),
                dma, dma((S, 2, PARTS)), dma, dma((S, 2, PARTS)),
                dma, dma((S - 1, 2, PIECES)), dma, dma((2, PIECES)), dma, dma((S - 1, 2, PIECES)), dma, dma((S, 2, PIECES)),
            ],
            compiler_params=pltpu.CompilerParams(
                collective_id=0, has_side_effects=True, vmem_limit_bytes=60 * 2**20,
            ),
            cost_estimate=pl.CostEstimate(flops=flops, bytes_accessed=4 * R * D * 2, transcendentals=R * R * 3),
        )(doc_lengths, queries, key_rows.T, value_rows.T, out_grad)
        query_grad, key_grad, value_grad = pl.pallas_call(
            hand_over, out_shape=shapes, in_specs=[hbm] * 3, out_specs=(hbm,) * 3, scratch_shapes=[dma((3,))],
            compiler_params=pltpu.CompilerParams(vmem_limit_bytes=2 * 2**20),
        )(*grads)
        return query_grad, key_grad.T, value_grad.T

    specs = (P("blk", "head"),) * 4 + (P(),)
    return jax.shard_map(shards, mesh=mesh, in_specs=specs, out_specs=specs[:3], check_vma=False)
```

time: 33.1 us -> 31.5 us (0.952)
  Pallas kernels: 32.3 us -> 30.7 us
    pallas_call x1, Pallas kernels: 31.6 us -> 30 us  [shards(): pl.pallas_call(functools.partial(kernel, blocks), out_shape=tuple((vmem(x...]
where the time goes in v3:
time: 31.5 us; the launch traced here: 31.4 us
  Pallas kernels  30.7 us (97%)
  between operations  0.64 us (2%)
    pallas_call x1, Pallas kernels, shards(): pl.pallas_call(functools.partial(kernel, blocks), out_shape=tuple((vmem(x...  30 us
    pallas_call x1, Pallas kernels, shards(): pl.pallas_call(hand_over, out_shape=shapes, in_specs=[hbm] * 3, out_specs...  0.73 us

profile of v3, /device:TPU:8, one launch (start us, length us, event | category | flops | bytes accessed | tf_op | source)
XLA Modules:
  0.0 31.4 jit_solution(18431454691197948310)
XLA Ops:
  0.6 30.0 %shard_map.76 = (bf16[768,128]{1,0:T(8,128)(2,1)S(1)}, bf16[32,768]{1,0:T(8,128)(2,1)S(1)}, bf16[32,768]{1,0:T(8,128)(2,1)S(1)}) custom-call(s32[16]{0:T(128)} %doc_hbm.1, bf16[768,128]{1,0:T(8,128)(2,1)} %q_hbm.1, bf16[32,768]{1,0:T(8,128)(2,1)} %bitcast.4, bf16[32,768]{1,0:T(8,128)(2,1)} %bitcast.5, bf16[768,128]{1,0:T(8,128)(2,1)} %do_hbm.1), custom_call_target="tpu_custom_call" | custom-call | flops 2113929216 | bytes 786432 | tf_op jit(solution)/shard_map/pallas_call | solution.py:384
  30.6 0.7 %shard_map.77 = (bf16[768,128]{1,0:T(8,128)(2,1)}, bf16[32,768]{1,0:T(8,128)(2,1)}, bf16[32,768]{1,0:T(8,128)(2,1)}) custom-call(bf16[768,128]{1,0:T(8,128)(2,1)S(1)} %get-tuple-element.9.refs_0_, bf16[32,768]{1,0:T(8,128)(2,1)S(1)} %get-tuple-element.10.refs_1_, bf16[32,768]{1,0:T(8,128)(2,1)S(1)} %get-tuple-element.11.refs_2_), custom_call_target="tpu_custom_call" | custom-call | tf_op jit(solution)/shard_map/pallas_call | solution.py:408
